TPU v7x, 256 devices: a whole 4x4x8 slice. The times are simulated.
256 devices in a mesh: dp: 64 (over z_lo, y, x), mp: 4 (over z_hi, core).
Axes of the slice: x: 4, y: 4, z: 8 (z_hi: 2, z_lo: 4; z = z_hi * 4 + z_lo), core: 2. Of those that a mesh axis runs over, the one named last changes fastest.
Arguments:
- view_one: bfloat16 [8192, 4096], P('dp', 'mp'), may hold values from -400 to 400
- view_two: bfloat16 [8192, 4096], P('dp', 'mp'), may hold values from -400 to 400
- proj_weight: bfloat16 [4096, 4096], P(None, 'mp'), may hold values from -0.09375 to 0.09375
Outputs:
- grad_one: bfloat16 [8192, 4096], P('dp', 'mp')
- grad_two: bfloat16 [8192, 4096], P('dp', 'mp')
All inputs are finite; a program needn't handle non-finite values.
Results may differ from a plain program's by a relative error of at most 0.025.
Values may be sent and summed in bfloat16 or wider, within the bound.
No kernel may reach another device: no remote copies, remote signals or barrier semaphores. Data moves between devices by JAX's collectives and lax.ppermute only.
A program may use at most 128 MiB of HBM per device.

v0:
```python
import jax
import jax.numpy as jnp
from jax import lax
from jax.sharding import PartitionSpec as P

OFF_WEIGHT = 0.0125
EPSILON = 1e-05


def contract_rows(left, right):
    return lax.dot_general(
        left, right, (((0,), (0,)), ((), ())), preferred_element_type=jnp.float32
    )


def times_transposed(left, right):
    return lax.dot_general(
        left, right, (((1,), (1,)), ((), ())), preferred_element_type=jnp.float32
    )


def local(view_one, view_two, proj_weight):
    row_count, local_width = view_one.shape
    batch_devices = lax.axis_size("dp")
    total_rows = row_count * batch_devices
    first = view_one.astype(jnp.float32)
    second = view_two.astype(jnp.float32)
    sum_one, sum_two = lax.psum((jnp.sum(first, axis=0), jnp.sum(second, axis=0)), "dp")
    center_one = sum_one / total_rows
    center_two = sum_two / total_rows
    centered_one = first - center_one
    centered_two = second - center_two
    square_one, square_two = lax.psum(
        (
            jnp.sum(centered_one * centered_one, axis=0),
            jnp.sum(centered_two * centered_two, axis=0),
        ),
        "dp",
    )
    variance_one = square_one / total_rows
    variance_two = square_two / total_rows
    inverse_one = lax.rsqrt(variance_one + EPSILON)
    inverse_two = lax.rsqrt(variance_two + EPSILON)
    norm_one = (centered_one * inverse_one).astype(jnp.bfloat16)
    norm_two = (centered_two * inverse_two).astype(jnp.bfloat16)
    whole_two = lax.all_gather(norm_two, "mp", axis=1, tiled=True)
    total_width = whole_two.shape[1]
    block_index = lax.axis_index("mp")
    slab_index = lax.axis_index("dp")
    shard_cols = total_width // batch_devices
    corr_part = contract_rows(norm_one, whole_two)
    corr_shard = lax.psum_scatter(corr_part, "dp", scatter_dimension=1, tiled=True) / total_rows
    row_ids = block_index * local_width + lax.broadcasted_iota(
        jnp.int32, (local_width, shard_cols), 0
    )
    col_ids = slab_index * shard_cols + lax.broadcasted_iota(
        jnp.int32, (local_width, shard_cols), 1
    )
    grad_shard = jnp.where(
        row_ids == col_ids, -2.0 * (1.0 - corr_shard), 2.0 * OFF_WEIGHT * corr_shard
    ).astype(jnp.bfloat16)
    piece = lax.all_gather(grad_shard, "dp", axis=1, tiled=True)
    upper = times_transposed(whole_two, piece)
    fresh = jnp.dot(norm_one, piece, preferred_element_type=jnp.float32)
    up_two = lax.psum_scatter(
        fresh.astype(jnp.bfloat16), "mp", scatter_dimension=1, tiled=True
    ).astype(jnp.float32)
    normal_one = norm_one.astype(jnp.float32)
    normal_two = norm_two.astype(jnp.float32)
    mean_up_one, cross_one, mean_up_two, cross_two = lax.psum(
        (
            jnp.sum(upper, axis=0),
            jnp.sum(upper * normal_one, axis=0),
            jnp.sum(up_two, axis=0),
            jnp.sum(up_two * normal_two, axis=0),
        ),
        "dp",
    )
    delta_one = (
        inverse_one * (upper - mean_up_one / total_rows - normal_one * (cross_one / total_rows))
    ).astype(jnp.bfloat16)
    delta_two = (
        inverse_two * (up_two - mean_up_two / total_rows - normal_two * (cross_two / total_rows))
    ).astype(jnp.bfloat16)
    partial_one = times_transposed(delta_one, proj_weight)
    partial_two = times_transposed(delta_two, proj_weight)
    summed_one, summed_two = (
        lax.psum_scatter(
            partial_one.astype(jnp.bfloat16), "mp", scatter_dimension=1, tiled=True
        ).astype(jnp.float32),
        lax.psum_scatter(
            partial_two.astype(jnp.bfloat16), "mp", scatter_dimension=1, tiled=True
        ).astype(jnp.float32),
    )
    return (summed_one.astype(jnp.bfloat16), summed_two.astype(jnp.bfloat16))


def solution(mesh):
    placed = (P("dp", "mp"), P("dp", "mp"), P(None, "mp"))
    return jax.shard_map(
        local, mesh=mesh, in_specs=placed, out_specs=(P("dp", "mp"), P("dp", "mp")), check_vma=False
    )
```

profile of v0, /device:TPU:1, one launch (start us, length us, event | category | flops | bytes accessed | tf_op | source)
XLA Modules:
  0.0 1705.4 jit_solution(12116241283504389625)
XLA Ops:
  7.2 0.0 all-gather.3.cloned.1.call-start
  7.2 1.0 convert_reduce_fusion.1
  8.2 1.0 convert_reduce_fusion.2
  9.2 165.1 %all-reduce.2 = (f32[1024]{0:T(1024)S(1)}, f32[1024]{0:T(1024)S(1)}) all-reduce(f32[1024]{0:T(1024)S(1)} %convert_reduce_fusion.1, f32[1024]{0:T(1024)S(1)} %convert_reduce_fusion.2), channel_id=1, replica_groups=mesh['dp'=64,'mp'=4] {'dp'}, use_global_device_ids=true, to_apply=%region_5.0 | all-reduce | flops 2048 | bytes 16384 | tf_op jit(solution)/shard_map/psum | solution.py:28
  174.4 1.0 fusion.6
  175.4 1.0 fusion.4
  176.5 155.3 %all-reduce.1 = (f32[1024]{0:T(1024)S(1)}, f32[1024]{0:T(1024)S(1)}) all-reduce(f32[1024]{0:T(1024)S(1)} %fusion.4, f32[1024]{0:T(1024)S(1)} %fusion.6), channel_id=1, replica_groups=mesh['dp'=64,'mp'=4] {'dp'}, use_global_device_ids=true, to_apply=%region_7.0 | all-reduce | flops 2048 | bytes 16384 | tf_op jit(solution)/shard_map/psum | solution.py:33
  331.8 1.7 fusion.5
  333.5 0.0 all-gather.3.cloned.1.call-update
  333.6 0.0 reduce-scatter.5.cloned.1.call-start
  333.6 84.8 %all-gather.3.cloned.1.call-done = bf16[128,4096]{1,0:T(8,128)(2,1)} async-done(((bf16[128,1024]{1,0:T(8,128)(2,1)}), bf16[128,4096]{1,0:T(8,128)(2,1)}) %all-gather.3.cloned.1.call-update) | async-done | bytes 1048592 | tf_op jit(solution)/shard_map/all_gather | solution.py:46
  418.4 9.4 fusion.26
  427.8 0.0 copy-start
  427.8 0.0 reduce-scatter.5.cloned.1.call-update
  427.8 0.0 copy-start.1
  427.8 0.0 all-gather.5.cloned.1.call-start
  427.9 355.8 %reduce-scatter.5.cloned.1.call-done = f32[1024,64]{0,1:T(8,128)} async-done(((f32[1024,4096]{0,1:T(8,128)}), f32[1024,64]{0,1:T(8,128)}) %reduce-scatter.5.cloned.1.call-update) | async-done | bytes 262160 | tf_op jit(solution)/shard_map/reduce_scatter | solution.py:52
  783.7 1.7 select_convert_fusion
  785.4 0.0 all-gather.5.cloned.1.call-update
  785.4 0.0 reduce-scatter.9.cloned.1.call-start
  785.5 366.2 %all-gather.5.cloned.1.call-done = bf16[1024,4096]{0,1:T(8,128)(2,1)} async-done(((bf16[1024,64]{0,1:T(8,128)(2,1)}), bf16[1024,4096]{0,1:T(8,128)(2,1)}) %all-gather.5.cloned.1.call-update) | async-done | bytes 8388624 | tf_op jit(solution)/shard_map/all_gather | solution.py:62
  1151.7 0.0 copy-done
  1151.7 7.3 convolution_convert_fusion.1
  1159.0 0.0 reduce-scatter.9.cloned.1.call-update
  1159.1 0.0 copy-start.2
  1159.1 0.0 copy-start.3
  1159.1 0.0 reduce-scatter.11.cloned.1.call-start
  1159.1 0.0 copy-done.1
  1159.1 4.7 fusion.28
  1163.9 77.9 %reduce-scatter.9.cloned.1.call-done = bf16[128,1024]{1,0:T(8,128)(2,1)} async-done(((bf16[128,4096]{1,0:T(8,128)(2,1)}), bf16[128,1024]{1,0:T(8,128)(2,1)}) %reduce-scatter.9.cloned.1.call-update) | async-done | bytes 262160 | tf_op jit(solution)/shard_map/reduce_scatter | solution.py:65
  1241.8 0.0 copy-done.2
  1241.8 1.1 convert_reduce_fusion
  1242.9 309.2 %all-reduce = (f32[1024]{0:T(1024)S(1)}, f32[1024]{0:T(1024)S(1)}, f32[1024]{0:T(1024)S(1)}, f32[1024]{0:T(1024)S(1)}) all-reduce(f32[1024]{0:T(1024)S(1)} %get-tuple-element.3, f32[1024]{0:T(1024)S(1)} %get-tuple-element.2, f32[1024]{0:T(1024)S(1)} %get-tuple-element.5, ...), channel_id=1, replica_groups=mesh['dp'=64,'mp'=4] {'dp'}, use_global_device_ids=true, to_apply=%region_12.13 | all-reduce | flops 4096 | bytes 32768 | tf_op jit(solution)/shard_map/psum | solution.py:70
  1552.0 0.0 copy-done.3
  1552.0 7.3 convolution_convert_fusion
  1559.4 0.0 reduce-scatter.11.cloned.1.call-update
  1559.4 0.0 reduce-scatter.7.cloned.1.call-start
  1559.5 7.3 convolution_convert_fusion.2
  1566.8 0.0 reduce-scatter.7.cloned.1.call-update
  1566.8 87.0 %reduce-scatter.11.cloned.1.call-done = bf16[128,1024]{1,0:T(8,128)(2,1)} async-done(((bf16[128,4096]{1,0:T(8,128)(2,1)}), bf16[128,1024]{1,0:T(8,128)(2,1)}) %reduce-scatter.11.cloned.1.call-update) | async-done | bytes 262160 | tf_op jit(solution)/shard_map/reduce_scatter | solution.py:91
  1653.8 44.8 %reduce-scatter.7.cloned.1.call-done = bf16[128,1024]{1,0:T(8,128)(2,1)} async-done(((bf16[128,4096]{1,0:T(8,128)(2,1)}), bf16[128,1024]{1,0:T(8,128)(2,1)}) %reduce-scatter.7.cloned.1.call-update) | async-done | bytes 262160 | tf_op jit(solution)/shard_map/reduce_scatter | solution.py:88
  (9 shorter events, 0.0 us)
Async XLA Ops:
  7.2 411.2 %all-gather.3.cloned.1.call-start = ((), (), s32[]{:S(2)}) async-start(), calls=%async_computation.4 | async-start | bytes 1310720 | tf_op jit(solution)/shard_map/all_gather | solution.py:46
  333.6 450.1 %reduce-scatter.5.cloned.1.call-start = ((), (), s32[]{:S(2)}) async-start(), calls=%async_computation.5 | async-start | bytes 17039360 | tf_op jit(solution)/shard_map/reduce_scatter | solution.py:52
  427.8 723.9 %copy-start = (bf16[128,1024]{1,0:T(8,128)(2,1)S(1)}, bf16[128,1024]{1,0:T(8,128)(2,1)}, u32[]{:S(2)}) copy-start(bf16[128,1024]{1,0:T(8,128)(2,1)} %param.3) | copy-start | bytes 786436
  427.8 731.3 %copy-start.1 = (bf16[128,4096]{1,0:T(8,128)(2,1)S(1)}, bf16[128,4096]{1,0:T(8,128)(2,1)}, u32[]{:S(2)}) copy-start(bf16[128,4096]{1,0:T(8,128)(2,1)} %all-gather.3.cloned.1.call-done) | copy-start | bytes 3145732
  427.8 723.9 %all-gather.5.cloned.1.call-start = ((), (), s32[]{:S(2)}) async-start(), calls=%async_computation.6 | async-start | bytes 8519680 | tf_op jit(solution)/shard_map/all_gather | solution.py:62
  785.4 456.4 %reduce-scatter.9.cloned.1.call-start = ((), (), s32[]{:S(2)}) async-start(), calls=%async_computation.8 | async-start | bytes 1310720 | tf_op jit(solution)/shard_map/reduce_scatter | solution.py:65
  1159.1 82.7 %copy-start.2 = (bf16[128,1024]{1,0:T(8,128)(2,1)S(1)}, bf16[128,1024]{1,0:T(8,128)(2,1)}, u32[]{:S(2)}) copy-start(bf16[128,1024]{1,0:T(8,128)(2,1)} %param.4) | copy-start | bytes 786436
  1159.1 393.0 %copy-start.3 = (bf16[128,1024]{1,0:T(8,128)(2,1)S(1)}, bf16[128,1024]{1,0:T(8,128)(2,1)}, u32[]{:S(2)}) copy-start(bf16[128,1024]{1,0:T(8,128)(2,1)} %fusion.5) | copy-start | bytes 786436
  1159.1 494.7 %reduce-scatter.11.cloned.1.call-start = ((), (), s32[]{:S(2)}) async-start(), calls=%async_computation.9 | async-start | bytes 1310720 | tf_op jit(solution)/shard_map/reduce_scatter | solution.py:91
  1559.4 139.1 %reduce-scatter.7.cloned.1.call-start = ((), (), s32[]{:S(2)}) async-start(), calls=%async_computation.7 | async-start | bytes 1310720 | tf_op jit(solution)/shard_map/reduce_scatter | solution.py:88
Sparse Core Ops, SparseCore 0:
  333.7 84.6 all-gather.2
  427.9 355.7 reduce-scatter.4
  786.1 365.5 all-gather.4
  1159.2 82.5 reduce-scatter.8
  1559.5 94.1 reduce-scatter.10
  1657.0 41.5 reduce-scatter.6
where the time goes:
time: 1710 us
  waiting for transfers between devices  1020 us (60%)
  blocking collectives  630 us (37%)
  matrix products  36.1 us (2%)
    all_gather x1, waiting for transfers between devices, local(): piece = lax.all_gather(grad_shard, 'dp', axis=1, tiled=True)  366 us
    reduce_scatter x1, waiting for transfers between devices, local(): lax.psum_scatter(corr_part, 'dp', scatter_dimension=1, tiled=True)  356 us
    psum x1, blocking collectives, local(): lax.psum((jnp.sum(upper, axis=0), jnp.sum(upper * normal_one, axis=0), jn...  309 us
    psum x1, blocking collectives, local(): lax.psum((jnp.sum(first, axis=0), jnp.sum(second, axis=0)), 'dp')  165 us
    psum x1, blocking collectives, local(): lax.psum((jnp.sum(centered_one * centered_one, axis=0), jnp.sum(centered_...  155 us
    reduce_scatter x1, waiting for transfers between devices, local(): lax.psum_scatter(partial_two.astype(jnp.bfloat16), 'mp', scatter_dimensio...  87 us
    all_gather x1, waiting for transfers between devices, local(): whole_two = lax.all_gather(norm_two, 'mp', axis=1, tiled=True)  84.8 us
    reduce_scatter x1, waiting for transfers between devices, local(): lax.psum_scatter(fresh.astype(jnp.bfloat16), 'mp', scatter_dimension=1, t...  77.9 us
  transfers between devices with their start and end apart: 6, of which 6 were waited for; matrix products, arithmetic and copies ran while one was open for 1% of the time, Pallas kernels for 0%

commit v1 on v0

v1 whole, which is shorter than its diff:
```python
import jax
import jax.numpy as jnp
from jax import lax
from jax.sharding import Mesh, PartitionSpec as P

OFF_WEIGHT = 0.0125
EPSILON = 1e-05
F32 = jnp.float32
BF16 = jnp.bfloat16
PLANE = ("y", "x")
SWAP = [(0, 1), (1, 0)]
EXTRA = 16


def dot(left, right, left_dim, right_dim):
    return lax.dot_general(
        left, right, (((left_dim,), (right_dim,)), ((), ())), preferred_element_type=F32
    )


def swap(value, axis):
    return lax.ppermute(value, axis, SWAP)


def gather_zl(value):
    count = lax.axis_size("zl")
    return lax.all_to_all(
        jnp.broadcast_to(value[None], (count,) + value.shape), "zl", 0, 0, tiled=True
    )


def small_gather_zl(value):
    count = lax.axis_size("zl")
    parts = [value]
    for shift in range(1, count):
        parts.append(lax.ppermute(value, "zl", [(i, (i + shift) % count) for i in range(count)]))
    return parts


def moments(values, total_rows):
    rows = values.shape[0]
    wide = values.astype(F32)
    mean = jnp.sum(wide, axis=0) / rows
    square = jnp.sum((wide - mean) ** 2, axis=0)
    parts = small_gather_zl(jnp.stack([mean, square]))
    center = sum(p[0] for p in parts) * (rows / total_rows)
    total = sum(p[1] + rows * (p[0] - center) ** 2 for p in parts)
    return center, lax.rsqrt(total / total_rows + EPSILON)


def split(vector):
    high = vector.astype(BF16)
    return high, (vector - high.astype(F32)).astype(BF16)


def extra_rows(vectors, width):
    rows = []
    for vector in vectors:
        rows.extend(split(vector))
    stacked = jnp.stack(rows)
    return jnp.pad(stacked, ((0, EXTRA - stacked.shape[0]), (0, 0)))


def local(view_one, view_two, proj_weight):
    rows, width = view_one.shape
    n_zl, n_y, n_x = lax.axis_size("zl"), lax.axis_size("y"), lax.axis_size("x")
    n_plane = n_y * n_x
    total_rows = rows * n_zl * n_plane
    blk_i, blk_j = width // n_x, width // n_y
    core = lax.axis_index("c")
    zh = lax.axis_index("zh")

    crossed = swap(view_two, "zh")
    send_one = view_one.reshape(rows, n_x, blk_i).transpose(1, 0, 2)
    send_one = jnp.broadcast_to(send_one[None], (n_y, n_x, rows, blk_i)).reshape(n_plane, rows, blk_i)
    own_one = lax.all_to_all(send_one, PLANE, 0, 0, tiled=True).reshape(n_plane * rows, blk_i)
    both = jnp.concatenate(
        [view_two.reshape(rows, n_y, blk_j), crossed.reshape(rows, n_y, blk_j)], axis=2
    ).transpose(1, 0, 2)
    both = jnp.broadcast_to(both[:, None], (n_y, n_x, rows, 2 * blk_j)).reshape(n_plane, rows, 2 * blk_j)
    plane_two = lax.all_to_all(both, PLANE, 0, 0, tiled=True).reshape(n_plane * rows, 2 * blk_j)
    plane_one = jnp.concatenate([own_one, swap(own_one, "c")], axis=1)

    mean_one, rstd_one = moments(plane_one, total_rows)
    mean_two, rstd_two = moments(plane_two, total_rows)
    norm_one = ((plane_one.astype(F32) - mean_one) * rstd_one).astype(BF16)
    norm_two = ((plane_two.astype(F32) - mean_two) * rstd_two).astype(BF16)

    tile_i, tile_j = norm_one.shape[1], norm_two.shape[1]
    part = dot(norm_one, norm_two, 0, 0).astype(BF16).reshape(n_zl, tile_i // n_zl, tile_j)
    sums = extra_rows(
        [jnp.sum(norm_one.astype(F32), axis=0), jnp.sum(norm_two.astype(F32), axis=0)], tile_j
    )
    part = jnp.concatenate([part, jnp.broadcast_to(sums[None], (n_zl,) + sums.shape)], axis=1)
    part = jnp.sum(lax.all_to_all(part, "zl", 0, 0, tiled=True).astype(F32), axis=0)
    slice_i = tile_i // n_zl
    mu_one = (part[slice_i] + part[slice_i + 1]) / total_rows
    mu_two = (part[slice_i + 2] + part[slice_i + 3]) / total_rows
    corr = part[:slice_i] / total_rows
    on_diag = lax.axis_index("x") == lax.axis_index("y")

    def diagonal(height, first):
        row_ids = first + lax.broadcasted_iota(jnp.int32, (height, tile_j), 0)
        col_ids = lax.broadcasted_iota(jnp.int32, (height, tile_j), 1)
        return (row_ids == col_ids) & (row_ids < blk_i) & on_diag

    grad = jnp.where(
        diagonal(slice_i, lax.axis_index("zl") * slice_i),
        -2.0 * (1.0 - corr),
        2.0 * OFF_WEIGHT * corr,
    ).astype(BF16)
    grad = gather_zl(grad).reshape(tile_i, tile_j)

    wide = grad.astype(F32)
    product = wide * jnp.where(diagonal(tile_i, 0), 1.0 + 0.5 * wide, wide / (2.0 * OFF_WEIGHT))
    cross_one, mean_up_one = jnp.sum(product, axis=1), jnp.sum(wide * mu_two[None, :], axis=1)
    cross_two, mean_up_two = jnp.sum(product, axis=0), jnp.sum(wide * mu_one[:, None], axis=0)

    def to_rows(upstream, vectors):
        columns = upstream.shape[1]
        extra = extra_rows(vectors, columns)
        slots = upstream.astype(BF16).reshape(n_plane, rows, columns)
        slots = jnp.concatenate([slots, jnp.broadcast_to(extra[None], (n_plane,) + extra.shape)], axis=1)
        return lax.all_to_all(slots, PLANE, 0, 0, tiled=True).reshape(n_y, n_x, rows + EXTRA, columns)

    up_two = dot(norm_one, grad, 1, 0)
    got_two = jnp.sum(to_rows(up_two, [cross_two, mean_up_two]).astype(F32), axis=1)
    cross_two = got_two[:, rows] + got_two[:, rows + 1]
    mean_up_two = got_two[:, rows + 2] + got_two[:, rows + 3]
    cross_sent = jnp.stack(
        split(cross_two[:, blk_j:]) + split(mean_up_two[:, blk_j:])
    ).reshape(4, width)
    up_two = got_two[:, :rows].transpose(1, 0, 2)
    sent = jnp.concatenate(
        [
            up_two[:, :, blk_j:].astype(BF16).reshape(rows, width),
            jnp.pad(cross_sent, ((0, EXTRA - 4), (0, 0))),
        ],
        axis=0,
    )
    sent = swap(sent, "zh").astype(F32)
    up_two = up_two[:, :, :blk_j].reshape(rows, width) + sent[:rows]
    cross_two = cross_two[:, :blk_j].reshape(width) + sent[rows] + sent[rows + 1]
    mean_up_two = mean_up_two[:, :blk_j].reshape(width) + sent[rows + 2] + sent[rows + 3]

    up_one = dot(norm_two, grad, 1, 1)
    other = jnp.concatenate(
        [
            up_one[:, blk_i:].astype(BF16),
            extra_rows([cross_one[blk_i:], mean_up_one[blk_i:]], blk_i),
        ],
        axis=0,
    )
    other = swap(other, "c").astype(F32)
    plane_rows = n_plane * rows
    up_one = up_one[:, :blk_i] + other[:plane_rows]
    tail = other[plane_rows:]
    cross_one = cross_one[:blk_i] + tail[0] + tail[1]
    mean_up_one = mean_up_one[:blk_i] + tail[2] + tail[3]
    got_one = jnp.sum(to_rows(up_one, [cross_one, mean_up_one]).astype(F32), axis=0)
    up_one = got_one[:, :rows].transpose(1, 0, 2).reshape(rows, width)
    cross_one = (got_one[:, rows] + got_one[:, rows + 1]).reshape(width)
    mean_up_one = (got_one[:, rows + 2] + got_one[:, rows + 3]).reshape(width)

    def own_stats(mean, rstd, axis):
        count = lax.axis_size(axis)
        return lax.all_to_all(
            jnp.broadcast_to(jnp.stack([mean, rstd])[None], (count, 2, mean.shape[0])), axis, 0, 0, tiled=True
        )

    stats_one = own_stats(mean_one[:blk_i], rstd_one[:blk_i], "x")
    stats_two = own_stats(mean_two[:blk_j], rstd_two[:blk_j], "y")

    def delta(view, stats, upstream, mean_up, cross):
        mean, rstd = stats[:, 0].reshape(width), stats[:, 1].reshape(width)
        normal = ((view.astype(F32) - mean) * rstd).astype(BF16).astype(F32)
        return (rstd * (upstream - mean_up - normal * cross)).astype(BF16)

    delta_one = delta(view_one, stats_one, up_one, mean_up_one, cross_one)
    delta_two = delta(view_two, stats_two, up_two, mean_up_two, cross_two)

    def input_grad(value):
        part = dot(value, proj_weight, 1, 1).reshape(rows, 2, 2, width)
        keep = lax.dynamic_index_in_dim(part, core, 2, keepdims=False)
        give = lax.dynamic_index_in_dim(part, 1 - core, 2, keepdims=False)
        part = keep + swap(give.astype(BF16), "c").astype(F32)
        keep = lax.dynamic_index_in_dim(part, zh, 1, keepdims=False)
        give = lax.dynamic_index_in_dim(part, 1 - zh, 1, keepdims=False)
        return (keep + swap(give.astype(BF16), "zh").astype(F32)).astype(BF16)

    return input_grad(delta_one), input_grad(delta_two)


def solution(mesh):
    fine = Mesh(mesh.devices.reshape(4, 4, 4, 2, 2), ("zl", "y", "x", "zh", "c"))
    spec = P(("zl", "y", "x"), ("zh", "c"))
    return jax.shard_map(
        local,
        mesh=fine,
        in_specs=(spec, spec, P(None, ("zh", "c"))),
        out_specs=(spec, spec),
        check_vma=False,
    )
```

time: 1710 us -> 295 us (0.17)
  waiting for transfers between devices: 1020 us -> 118 us
  blocking collectives: 630 us -> 0 us
  starting transfers between devices: 0.25 us -> 93.5 us
  local copies, waits for them, and re-layouts: 0.02 us -> 27.7 us
  other arithmetic: 8.64 us -> 28.8 us
    psum x3 -> x0, blocking collectives: 630 us -> none  [the longest x1 309 us: local(): lax.psum((jnp.sum(upper, axis=0), jnp.sum(upper * normal_one, axis=0), jn...]
    reduce_scatter x4 -> x0, waiting for transfers between devices: 565 us -> none  [the longest x1 356 us: local(): lax.psum_scatter(corr_part, 'dp', scatter_dimension=1, tiled=True)]
    all_gather x2 -> x0, waiting for transfers between devices: 451 us -> none  [the longest x1 366 us: local(): piece = lax.all_gather(grad_shard, 'dp', axis=1, tiled=True)]
    all_to_all x0 -> x8, waiting for transfers between devices: none -> 88.9 us  [the longest x2 33.4 us: to_rows(): lax.all_to_all(slots, PLANE, 0, 0, tiled=True)]
    ppermute x0 -> x14, starting transfers between devices: none -> 58.4 us  [the longest x8 41.1 us: swap(): return lax.ppermute(value, axis, SWAP)]
    all_to_all x0 -> x8, starting transfers between devices: none -> 35.1 us  [the longest x2 8.81 us: to_rows(): lax.all_to_all(slots, PLANE, 0, 0, tiled=True)]
    ppermute x0 -> x14, waiting for transfers between devices: none -> 28.9 us  [the longest x8 28.1 us: swap(): return lax.ppermute(value, axis, SWAP)]
  transfers between devices with their start and end apart: 6 -> 22, of which waited for: 6 -> 14; matrix products, arithmetic and copies ran while one was open for 1% -> 19% of each run, Pallas kernels for 0% -> 0%
where the time goes in v1:
time: 295 us; the launch traced here: 292 us
  waiting for transfers between devices  118 us (40%)
  starting transfers between devices  93.5 us (32%)
  other arithmetic  28.8 us (10%)
  local copies, waits for them, and re-layouts  27.7 us (9%)
  matrix products  22.8 us (8%)
    ppermute x8, starting transfers between devices, swap(): return lax.ppermute(value, axis, SWAP)  41.1 us
    all_to_all x2, waiting for transfers between devices, to_rows(): lax.all_to_all(slots, PLANE, 0, 0, tiled=True)  33.4 us
    ppermute x8, waiting for transfers between devices, swap(): return lax.ppermute(value, axis, SWAP)  28.1 us
    dot_general x5, matrix products, dot(): lax.dot_general(left, right, (((left_dim,), (right_dim,)), ((), ())), pre...  22.8 us
    all_to_all x1, waiting for transfers between devices, local(): lax.all_to_all(both, PLANE, 0, 0, tiled=True)  20.6 us
    ppermute x6, starting transfers between devices, small_gather_zl(): lax.ppermute(value, 'zl', [(i, (i + shift) % count) for i in range(count)])  17.4 us
    all_to_all x1, waiting for transfers between devices, local(): lax.all_to_all(part, 'zl', 0, 0, tiled=True).astype(F32)  14.6 us
    all_to_all x1, waiting for transfers between devices, gather_zl(): lax.all_to_all(jnp.broadcast_to(value[None], (count,) + value.shape), 'zl...  13.4 us
  transfers between devices with their start and end apart: 22, of which 14 were waited for; matrix products, arithmetic and copies ran while one was open for 19% of the time, Pallas kernels for 0%

profile of v1, /device:TPU:1, one launch (start us, length us, event | category | flops | bytes accessed | tf_op | source)
XLA Modules:
  0.0 292.4 jit_solution(9951865938343311551)
XLA Ops:
  0.6 1.2 reshape.339
  1.9 1.1 broadcast_in_dim.16
  3.0 7.6 %all-to-all-start = ((bf16[16,128,256]{2,1,0:T(8,128)(2,1)}), bf16[16,128,256]{2,1,0:T(8,128)(2,1)S(1)}, u32[]{:S(2)}, u32[]{:S(2)}) async-start(bf16[16,128,256]{2,1,0:T(8,128)(2,1)} %bitcast.1), calls=%async_computation | async-start | bytes 2097152 | tf_op jit(solution)/shard_map/all_to_all | solution.py:76
  10.6 7.0 %collective-permute-start.4 = (bf16[128,1024]{1,0:T(8,128)(2,1)S(1)}, bf16[128,1024]{1,0:T(8,128)(2,1)S(1)}, u32[]{:S(2)}, u32[]{:S(2)}) collective-permute-start(bf16[128,1024]{1,0:T(8,128)(2,1)S(1)} %copy-done.6), channel_id=1, source_target_pairs={{0,2},{2,0},{1,3},{3,1},{4,6},{6,4},{5,7},{7,5},{8,10},{10,8},{9,1... | collective-permute-start | bytes 786440 | tf_op jit(solution)/shard_map/ppermute | solution.py:22
  17.7 6.5 %collective-permute-done.4 = bf16[128,1024]{1,0:T(8,128)(2,1)S(1)} collective-permute-done((bf16[128,1024]{1,0:T(8,128)(2,1)S(1)}, bf16[128,1024]{1,0:T(8,128)(2,1)S(1)}, u32[]{:S(2)}, u32[]{:S(2)}) %collective-permute-start.4) | collective-permute-done | bytes 262176 | tf_op jit(solution)/shard_map/ppermute | solution.py:22
  24.4 2.1 all-to-all-done
  26.5 2.6 collective-permute-start
  29.5 1.5 broadcast_in_dim.18
  31.0 3.7 %all-to-all-start.2 = ((bf16[16,128,512]{2,1,0:T(8,128)(2,1)}), bf16[16,128,512]{2,1,0:T(8,128)(2,1)S(1)}, u32[]{:S(2)}, u32[]{:S(2)}) async-start(bf16[16,128,512]{2,1,0:T(8,128)(2,1)} %bitcast.158), calls=%async_computation.2 | async-start | bytes 4194304 | tf_op jit(solution)/shard_map/all_to_all | solution.py:81
  34.8 1.6 convert_reduce_fusion
  36.4 1.8 fusion.1
  38.2 5.4 %collective-permute-start.1 = (f32[2,512]{1,0:T(2,128)S(1)}, f32[2,512]{1,0:T(2,128)S(1)}, u32[]{:S(2)}, u32[]{:S(2)}) collective-permute-start(f32[2,512]{1,0:T(2,128)S(1)} %pad_maximum_fusion.6), channel_id=1, source_target_pairs={{0,64},{64,128},{128,192},{192,0},{1,65},{65,129},{129,193},{193,1... | collective-permute-start | bytes 12296 | tf_op jit(solution)/shard_map/ppermute | solution.py:36
  43.6 0.9 collective-permute-start.2
  44.5 2.3 collective-permute-start.3
  47.6 20.6 %all-to-all-done.2 = bf16[16,128,512]{2,1,0:T(8,128)(2,1)S(1)} async-done(((bf16[16,128,512]{2,1,0:T(8,128)(2,1)}), bf16[16,128,512]{2,1,0:T(8,128)(2,1)S(1)}, u32[]{:S(2)}, u32[]{:S(2)}) %all-to-all-start.2) | async-done | bytes 2097184 | tf_op jit(solution)/shard_map/all_to_all | solution.py:81
  69.1 5.4 %collective-permute-start.5 = (f32[2,512]{1,0:T(2,128)S(1)}, f32[2,512]{1,0:T(2,128)S(1)}, u32[]{:S(2)}, u32[]{:S(2)}) collective-permute-start(f32[2,512]{1,0:T(2,128)S(1)} %pad_maximum_fusion.7), channel_id=1, source_target_pairs={{0,64},{64,128},{128,192},{192,0},{1,65},{65,129},{129,193},{193,1... | collective-permute-start | bytes 12296 | tf_op jit(solution)/shard_map/ppermute | solution.py:36
  75.4 2.5 collective-permute-start.7
  77.9 1.8 convert_reduce_fusion.3
  79.8 2.1 convert_reduce_fusion.2
  82.5 2.5 convolution_convert_fusion.1
  85.9 4.3 %all-to-all-start.3 = ((bf16[4,144,512]{2,1,0:T(8,128)(2,1)}), bf16[4,144,512]{2,1,0:T(8,128)(2,1)}, u32[]{:S(2)}, u32[]{:S(2)}) async-start(bf16[4,144,512]{2,1,0:T(8,128)(2,1)} %pad_maximum_fusion.4), calls=%async_computation.3 | async-start | bytes 1179648 | tf_op jit(solution)/shard_map/all_to_all | solution.py:95
  90.2 14.6 %all-to-all-done.3 = bf16[4,144,512]{2,1,0:T(8,128)(2,1)} async-done(((bf16[4,144,512]{2,1,0:T(8,128)(2,1)}), bf16[4,144,512]{2,1,0:T(8,128)(2,1)}, u32[]{:S(2)}, u32[]{:S(2)}) %all-to-all-start.3) | async-done | bytes 589856 | tf_op jit(solution)/shard_map/all_to_all | solution.py:95
  104.8 1.2 convert_reduce_fusion.6
  107.0 4.2 %all-to-all-start.4 = ((bf16[4,128,512]{2,1,0:T(8,128)(2,1)}), bf16[4,128,512]{2,1,0:T(8,128)(2,1)}, u32[]{:S(2)}, u32[]{:S(2)}) async-start(bf16[4,128,512]{2,1,0:T(8,128)(2,1)} %broadcast_in_dim.20), calls=%async_computation.4 | async-start | bytes 1048576 | tf_op jit(solution)/shard_map/all_to_all | solution.py:27
  111.2 13.4 %all-to-all-done.4 = bf16[4,128,512]{2,1,0:T(8,128)(2,1)} async-done(((bf16[4,128,512]{2,1,0:T(8,128)(2,1)}), bf16[4,128,512]{2,1,0:T(8,128)(2,1)}, u32[]{:S(2)}, u32[]{:S(2)}) %all-to-all-start.4) | async-done | bytes 524320 | tf_op jit(solution)/shard_map/all_to_all | solution.py:27
  124.6 2.5 fusion.16
  127.2 2.4 fusion.78
  129.6 1.9 copy-done
  131.8 2.2 collective-permute-start.8
  134.6 3.2 %all-to-all-start.1 = ((f32[4,2,256]{2,1,0:T(2,128)}), f32[4,2,256]{2,1,0:T(2,128)S(1)}, u32[]{:S(2)}, u32[]{:S(2)}) async-start(f32[4,2,256]{2,1,0:T(2,128)} %broadcast_in_dim.17), calls=%async_computation.1 | async-start | bytes 16384 | tf_op jit(solution)/shard_map/all_to_all | solution.py:167
  138.1 1.9 fusion.6
  140.0 2.0 all-to-all-done.1
  142.6 3.2 %all-to-all-start.6 = ((f32[4,2,256]{2,1,0:T(2,128)}), f32[4,2,256]{2,1,0:T(2,128)S(1)}, u32[]{:S(2)}, u32[]{:S(2)}) async-start(f32[4,2,256]{2,1,0:T(2,128)} %broadcast_in_dim.22), calls=%async_computation.6 | async-start | bytes 16384 | tf_op jit(solution)/shard_map/all_to_all | solution.py:167
  145.9 1.1 pad_maximum_fusion.2
  147.0 2.9 %all-to-all-done.6 = f32[4,2,256]{2,1,0:T(2,128)S(1)} async-done(((f32[4,2,256]{2,1,0:T(2,128)}), f32[4,2,256]{2,1,0:T(2,128)S(1)}, u32[]{:S(2)}, u32[]{:S(2)}) %all-to-all-start.6) | async-done | bytes 8224 | tf_op jit(solution)/shard_map/all_to_all | solution.py:167
  150.0 3.7 %all-to-all-start.5 = ((bf16[16,144,256]{2,1,0:T(8,128)(2,1)}), bf16[16,144,256]{2,1,0:T(8,128)(2,1)S(1)}, u32[]{:S(2)}, u32[]{:S(2)}) async-start(bf16[16,144,256]{2,1,0:T(8,128)(2,1)} %pad_maximum_fusion.2), calls=%async_computation.5 | async-start | bytes 2359296 | tf_op jit(solution)/shard_map/all_to_all | solution.py:124
  153.8 2.6 convolution_convert_fusion
  156.5 1.6 pad_maximum_fusion
  158.1 11.7 %all-to-all-done.5 = bf16[16,144,256]{2,1,0:T(8,128)(2,1)S(1)} async-done(((bf16[16,144,256]{2,1,0:T(8,128)(2,1)}), bf16[16,144,256]{2,1,0:T(8,128)(2,1)S(1)}, u32[]{:S(2)}, u32[]{:S(2)}) %all-to-all-start.5) | async-done | bytes 1179680 | tf_op jit(solution)/shard_map/all_to_all | solution.py:124
  169.8 5.1 %all-to-all-start.7 = ((bf16[16,144,512]{2,1,0:T(8,128)(2,1)}), bf16[16,144,512]{2,1,0:T(8,128)(2,1)S(1)}, u32[]{:S(2)}, u32[]{:S(2)}) async-start(bf16[16,144,512]{2,1,0:T(8,128)(2,1)} %pad_maximum_fusion), calls=%async_computation.7 | async-start | bytes 4718592 | tf_op jit(solution)/shard_map/all_to_all | solution.py:124
  174.9 1.8 copy.75
  176.7 1.8 copy.68
  180.4 1.0 slice_add_fusion.5
  181.3 1.6 fusion.33
  183.0 21.7 %all-to-all-done.7 = bf16[16,144,512]{2,1,0:T(8,128)(2,1)S(1)} async-done(((bf16[16,144,512]{2,1,0:T(8,128)(2,1)}), bf16[16,144,512]{2,1,0:T(8,128)(2,1)S(1)}, u32[]{:S(2)}, u32[]{:S(2)}) %all-to-all-start.7) | async-done | bytes 2359328 | tf_op jit(solution)/shard_map/all_to_all | solution.py:124
  207.5 15.8 %collective-permute-start.11 = (bf16[144,1024]{0,1:T(8,128)(2,1)}, bf16[144,1024]{0,1:T(8,128)(2,1)}, u32[]{:S(2)}, u32[]{:S(2)}) collective-permute-start(bf16[144,1024]{0,1:T(8,128)(2,1)} %fusion.18), channel_id=1, source_target_pairs={{0,2},{2,0},{1,3},{3,1},{4,6},{6,4},{5,7},{7,5},{8,10},{10,8},{9,1... | collective-permute-start | bytes 884744 | tf_op jit(solution)/shard_map/ppermute | solution.py:22
  223.3 7.6 %fusion.79 = f32[128,4096]{1,0:T(8,128)} fusion(bf16[128,1024]{0,1:T(8,128)(2,1)S(1)} %fusion.33, bf16[4096,1024]{1,0:T(8,128)(2,1)} %param.5), kind=kOutput, calls=%fused_computation.176 | convolution fusion | flops 1073741824 | bytes 10747904 | tf_op jit(solution)/shard_map/dot_general | solution.py:16
  231.0 3.0 %reshape.349 = f32[128,2,2,1024]{3,2,1,0:T(2,128)S(1)} reshape(f32[128,4096]{1,0:T(8,128)} %fusion.79) | data formatting | bytes 4194304 | tf_op jit(solution)/shard_map/reshape | solution.py:183
  234.0 1.1 constant_dynamic-slice_fusion.2
  235.1 1.1 copy.101
  236.2 5.2 %collective-permute-start.9 = (bf16[128,2,1024]{2,0,1:T(8,128)(2,1)}, bf16[128,2,1024]{2,0,1:T(8,128)(2,1)}, u32[]{:S(2)}, u32[]{:S(2)}) collective-permute-start(bf16[128,2,1024]{2,0,1:T(8,128)(2,1)} %bitcast.147), channel_id=1, source_target_pairs={{0,1},{1,0},{2,3},{3,2},{4,5},{5,4},{6,7},{7,6},{8,9},{9,8},{10,11... | collective-permute-start | bytes 1572872 | tf_op jit(solution)/shard_map/ppermute | solution.py:22
  241.4 1.1 constant_dynamic-slice_fusion.3
  243.2 2.5 collective-permute-done.11
  245.8 1.1 convert_element_type.448
  248.3 7.6 %fusion.80 = f32[128,4096]{1,0:T(8,128)} fusion(bf16[128,1024]{0,1:T(8,128)(2,1)S(1)} %fusion.28, bf16[4096,1024]{1,0:T(8,128)(2,1)} %param.5), kind=kOutput, calls=%fused_computation.177 | convolution fusion | flops 1073741824 | bytes 10747904 | tf_op jit(solution)/shard_map/dot_general | solution.py:16
  255.9 3.0 %reshape.355 = f32[128,2,2,1024]{3,2,1,0:T(2,128)S(1)} reshape(f32[128,4096]{1,0:T(8,128)} %fusion.80) | data formatting | bytes 4194304 | tf_op jit(solution)/shard_map/reshape | solution.py:183
  259.0 1.1 constant_dynamic-slice_fusion
  260.4 2.7 collective-permute-start.12
  263.1 1.1 constant_dynamic-slice_fusion.1
  264.2 1.4 bitcast_add_fusion.1
  265.6 2.4 collective-permute-start.10
  268.5 3.1 %collective-permute-start.13 = (bf16[128,1024]{1,0:T(8,128)(2,1)S(1)}, bf16[128,1024]{1,0:T(8,128)(2,1)S(1)}, u32[]{:S(2)}, u32[]{:S(2)}) collective-permute-start(bf16[128,1024]{1,0:T(8,128)(2,1)S(1)} %fusion.35), channel_id=1, source_target_pairs={{0,2},{2,0},{1,3},{3,1},{4,6},{6,4},{5,7},{7,5},{8,10},{10,8},{9,1... | collective-permute-start | bytes 786440 | tf_op jit(solution)/shard_map/ppermute | solution.py:22
  271.6 14.2 %collective-permute-done.10 = bf16[128,1024]{1,0:T(8,128)(2,1)S(1)} collective-permute-done((bf16[128,1024]{1,0:T(8,128)(2,1)S(1)}, bf16[128,1024]{1,0:T(8,128)(2,1)S(1)}, u32[]{:S(2)}, u32[]{:S(2)}) %collective-permute-start.10) | collective-permute-done | bytes 262176 | tf_op jit(solution)/shard_map/ppermute | solution.py:22
  286.6 4.9 %collective-permute-done.13 = bf16[128,1024]{1,0:T(8,128)(2,1)S(1)} collective-permute-done((bf16[128,1024]{1,0:T(8,128)(2,1)S(1)}, bf16[128,1024]{1,0:T(8,128)(2,1)S(1)}, u32[]{:S(2)}, u32[]{:S(2)}) %collective-permute-start.13) | collective-permute-done | bytes 262176 | tf_op jit(solution)/shard_map/ppermute | solution.py:22
  (135 shorter events, 16.6 us)
Async XLA Ops:
  0.6 9.9 %copy-start.6 = (bf16[128,1024]{1,0:T(8,128)(2,1)S(1)}, bf16[128,1024]{1,0:T(8,128)(2,1)}, u32[]{:S(2)}) copy-start(bf16[128,1024]{1,0:T(8,128)(2,1)} %param.4) | copy-start | bytes 786436
  3.0 23.6 %all-to-all-start = ((bf16[16,128,256]{2,1,0:T(8,128)(2,1)}), bf16[16,128,256]{2,1,0:T(8,128)(2,1)S(1)}, u32[]{:S(2)}, u32[]{:S(2)}) async-start(bf16[16,128,256]{2,1,0:T(8,128)(2,1)} %bitcast.1), calls=%async_computation | async-start | bytes 2097152 | tf_op jit(solution)/shard_map/all_to_all | solution.py:76
  10.6 13.7 %collective-permute-start.4 = (bf16[128,1024]{1,0:T(8,128)(2,1)S(1)}, bf16[128,1024]{1,0:T(8,128)(2,1)S(1)}, u32[]{:S(2)}, u32[]{:S(2)}) collective-permute-start(bf16[128,1024]{1,0:T(8,128)(2,1)S(1)} %copy-done.6), channel_id=1, source_target_pairs={{0,2},{2,0},{1,3},{3,1},{4,6},{6,4},{5,7},{7,5},{8,10},{10,8},{9,1... | collective-permute-start | bytes 786440 | tf_op jit(solution)/shard_map/ppermute | solution.py:22
  26.5 8.2 %collective-permute-start = (bf16[2048,256]{1,0:T(8,128)(2,1)S(1)}, bf16[2048,256]{1,0:T(8,128)(2,1)}, u32[]{:S(2)}, u32[]{:S(2)}) collective-permute-start(bf16[2048,256]{1,0:T(8,128)(2,1)S(1)} %bitcast.151), channel_id=1, source_target_pairs={{0,1},{1,0},{2,3},{3,2},{4,5},{5,4},{6,7},{7,6},{8,9},{9,8},{10,11... | collective-permute-start | bytes 3145736 | tf_op jit(solution)/shard_map/ppermute | solution.py:22
  31.0 37.1 %all-to-all-start.2 = ((bf16[16,128,512]{2,1,0:T(8,128)(2,1)}), bf16[16,128,512]{2,1,0:T(8,128)(2,1)S(1)}, u32[]{:S(2)}, u32[]{:S(2)}) async-start(bf16[16,128,512]{2,1,0:T(8,128)(2,1)} %bitcast.158), calls=%async_computation.2 | async-start | bytes 4194304 | tf_op jit(solution)/shard_map/all_to_all | solution.py:81
  38.2 8.6 %collective-permute-start.1 = (f32[2,512]{1,0:T(2,128)S(1)}, f32[2,512]{1,0:T(2,128)S(1)}, u32[]{:S(2)}, u32[]{:S(2)}) collective-permute-start(f32[2,512]{1,0:T(2,128)S(1)} %pad_maximum_fusion.6), channel_id=1, source_target_pairs={{0,64},{64,128},{128,192},{192,0},{1,65},{65,129},{129,193},{193,1... | collective-permute-start | bytes 12296 | tf_op jit(solution)/shard_map/ppermute | solution.py:36
  43.6 3.7 %collective-permute-start.2 = (f32[2,512]{1,0:T(2,128)S(1)}, f32[2,512]{1,0:T(2,128)S(1)}, u32[]{:S(2)}, u32[]{:S(2)}) collective-permute-start(f32[2,512]{1,0:T(2,128)S(1)} %pad_maximum_fusion.6), channel_id=1, source_target_pairs={{0,128},{64,192},{128,0},{192,64},{1,129},{65,193},{129,1},{193,65... | collective-permute-start | bytes 12296 | tf_op jit(solution)/shard_map/ppermute | solution.py:36
  44.5 3.0 %collective-permute-start.3 = (f32[2,512]{1,0:T(2,128)S(1)}, f32[2,512]{1,0:T(2,128)S(1)}, u32[]{:S(2)}, u32[]{:S(2)}) collective-permute-start(f32[2,512]{1,0:T(2,128)S(1)} %pad_maximum_fusion.6), channel_id=1, source_target_pairs={{0,192},{64,0},{128,64},{192,128},{1,193},{65,1},{129,65},{193,129... | collective-permute-start | bytes 12296 | tf_op jit(solution)/shard_map/ppermute | solution.py:36
  47.5 34.9 %copy-start.11 = (f32[1,512]{1,0:T(1,128)}, f32[1,512]{1,0:T(1,128)S(1)}, u32[]{:S(2)}) copy-start(f32[1,512]{1,0:T(1,128)S(1)} %get-tuple-element.12) | copy-start | bytes 6148
  47.6 34.9 %copy-start.13 = (f32[1,512]{1,0:T(1,128)}, f32[1,512]{1,0:T(1,128)S(1)}, u32[]{:S(2)}) copy-start(f32[1,512]{1,0:T(1,128)S(1)} %get-tuple-element.13) | copy-start | bytes 6148
  69.1 10.6 %collective-permute-start.5 = (f32[2,512]{1,0:T(2,128)S(1)}, f32[2,512]{1,0:T(2,128)S(1)}, u32[]{:S(2)}, u32[]{:S(2)}) collective-permute-start(f32[2,512]{1,0:T(2,128)S(1)} %pad_maximum_fusion.7), channel_id=1, source_target_pairs={{0,64},{64,128},{128,192},{192,0},{1,65},{65,129},{129,193},{193,1... | collective-permute-start | bytes 12296 | tf_op jit(solution)/shard_map/ppermute | solution.py:36
  74.5 5.3 %collective-permute-start.6 = (f32[2,512]{1,0:T(2,128)S(1)}, f32[2,512]{1,0:T(2,128)S(1)}, u32[]{:S(2)}, u32[]{:S(2)}) collective-permute-start(f32[2,512]{1,0:T(2,128)S(1)} %pad_maximum_fusion.7), channel_id=1, source_target_pairs={{0,128},{64,192},{128,0},{192,64},{1,129},{65,193},{129,1},{193,65... | collective-permute-start | bytes 12296 | tf_op jit(solution)/shard_map/ppermute | solution.py:36
  75.4 4.4 %collective-permute-start.7 = (f32[2,512]{1,0:T(2,128)S(1)}, f32[2,512]{1,0:T(2,128)S(1)}, u32[]{:S(2)}, u32[]{:S(2)}) collective-permute-start(f32[2,512]{1,0:T(2,128)S(1)} %pad_maximum_fusion.7), channel_id=1, source_target_pairs={{0,192},{64,0},{128,64},{192,128},{1,193},{65,1},{129,65},{193,129... | collective-permute-start | bytes 12296 | tf_op jit(solution)/shard_map/ppermute | solution.py:36
  85.9 41.3 %copy-start.1 = (bf16[16,128,512]{2,1,0:T(8,128)(2,1)S(1)}, bf16[16,128,512]{2,1,0:T(8,128)(2,1)}, u32[]{:S(2)}) copy-start(bf16[16,128,512]{2,1,0:T(8,128)(2,1)} %get-tuple-element.15) | copy-start | bytes 6291460
  85.9 18.9 %all-to-all-start.3 = ((bf16[4,144,512]{2,1,0:T(8,128)(2,1)}), bf16[4,144,512]{2,1,0:T(8,128)(2,1)}, u32[]{:S(2)}, u32[]{:S(2)}) async-start(bf16[4,144,512]{2,1,0:T(8,128)(2,1)} %pad_maximum_fusion.4), calls=%async_computation.3 | async-start | bytes 1179648 | tf_op jit(solution)/shard_map/all_to_all | solution.py:95
  107.0 17.6 %all-to-all-start.4 = ((bf16[4,128,512]{2,1,0:T(8,128)(2,1)}), bf16[4,128,512]{2,1,0:T(8,128)(2,1)}, u32[]{:S(2)}, u32[]{:S(2)}) async-start(bf16[4,128,512]{2,1,0:T(8,128)(2,1)} %broadcast_in_dim.20), calls=%async_computation.4 | async-start | bytes 1048576 | tf_op jit(solution)/shard_map/all_to_all | solution.py:27
  129.6 2.0 copy-start
  131.8 6.2 %collective-permute-start.8 = (bf16[2064,256]{1,0:T(8,128)(2,1)S(1)}, bf16[2064,256]{1,0:T(8,128)(2,1)S(1)}, u32[]{:S(2)}, u32[]{:S(2)}) collective-permute-start(bf16[2064,256]{1,0:T(8,128)(2,1)S(1)} %pad_maximum_fusion.3), channel_id=1, source_target_pairs={{0,1},{1,0},{2,3},{3,2},{4,5},{5,4},{6,7},{7,6},{8,9},{9,8},{10,11... | collective-permute-start | bytes 3170312 | tf_op jit(solution)/shard_map/ppermute | solution.py:22
  134.6 7.4 %all-to-all-start.1 = ((f32[4,2,256]{2,1,0:T(2,128)}), f32[4,2,256]{2,1,0:T(2,128)S(1)}, u32[]{:S(2)}, u32[]{:S(2)}) async-start(f32[4,2,256]{2,1,0:T(2,128)} %broadcast_in_dim.17), calls=%async_computation.1 | async-start | bytes 16384 | tf_op jit(solution)/shard_map/all_to_all | solution.py:167
  142.6 7.4 %all-to-all-start.6 = ((f32[4,2,256]{2,1,0:T(2,128)}), f32[4,2,256]{2,1,0:T(2,128)S(1)}, u32[]{:S(2)}, u32[]{:S(2)}) async-start(f32[4,2,256]{2,1,0:T(2,128)} %broadcast_in_dim.22), calls=%async_computation.6 | async-start | bytes 16384 | tf_op jit(solution)/shard_map/all_to_all | solution.py:167
  145.9 7.8 %copy-start.7 = (f32[512]{0:T(512)S(1)}, f32[512]{0:T(512)}, u32[]{:S(2)}) copy-start(f32[512]{0:T(512)} %get-tuple-element.4) | copy-start | bytes 6148
  145.9 7.8 %copy-start.8 = (f32[512]{0:T(512)S(1)}, f32[512]{0:T(512)}, u32[]{:S(2)}) copy-start(f32[512]{0:T(512)} %get-tuple-element.7) | copy-start | bytes 6148
  145.9 7.9 %copy-start.12 = (f32[1,512]{1,0:T(1,128)S(1)}, f32[1,512]{1,0:T(1,128)}, u32[]{:S(2)}) copy-start(f32[1,512]{1,0:T(1,128)} %copy-done.11) | copy-start | bytes 6148
  145.9 7.9 %copy-start.14 = (f32[1,512]{1,0:T(1,128)S(1)}, f32[1,512]{1,0:T(1,128)}, u32[]{:S(2)}) copy-start(f32[1,512]{1,0:T(1,128)} %copy-done.13) | copy-start | bytes 6148
  150.0 19.8 %all-to-all-start.5 = ((bf16[16,144,256]{2,1,0:T(8,128)(2,1)}), bf16[16,144,256]{2,1,0:T(8,128)(2,1)S(1)}, u32[]{:S(2)}, u32[]{:S(2)}) async-start(bf16[16,144,256]{2,1,0:T(8,128)(2,1)} %pad_maximum_fusion.2), calls=%async_computation.5 | async-start | bytes 2359296 | tf_op jit(solution)/shard_map/all_to_all | solution.py:124
  169.8 34.9 %all-to-all-start.7 = ((bf16[16,144,512]{2,1,0:T(8,128)(2,1)}), bf16[16,144,512]{2,1,0:T(8,128)(2,1)S(1)}, u32[]{:S(2)}, u32[]{:S(2)}) async-start(bf16[16,144,512]{2,1,0:T(8,128)(2,1)} %pad_maximum_fusion), calls=%async_computation.7 | async-start | bytes 4718592 | tf_op jit(solution)/shard_map/all_to_all | solution.py:124
  179.1 2.2 copy-start.9
  179.1 2.2 copy-start.10
  179.3 0.8 copy-start.4
  205.1 1.0 copy-start.2
  207.5 38.2 %collective-permute-start.11 = (bf16[144,1024]{0,1:T(8,128)(2,1)}, bf16[144,1024]{0,1:T(8,128)(2,1)}, u32[]{:S(2)}, u32[]{:S(2)}) collective-permute-start(bf16[144,1024]{0,1:T(8,128)(2,1)} %fusion.18), channel_id=1, source_target_pairs={{0,2},{2,0},{1,3},{3,1},{4,6},{6,4},{5,7},{7,5},{8,10},{10,8},{9,1... | collective-permute-start | bytes 884744 | tf_op jit(solution)/shard_map/ppermute | solution.py:22
  235.1 7.4 %copy-start.3 = (f32[128,4,512]{2,0,1:T(8,128)S(1)}, f32[128,4,512]{2,0,1:T(8,128)}, u32[]{:S(2)}) copy-start(f32[128,4,512]{2,0,1:T(8,128)} %copy-done.2) | copy-start | bytes 3145732
  236.2 28.0 %collective-permute-start.9 = (bf16[128,2,1024]{2,0,1:T(8,128)(2,1)}, bf16[128,2,1024]{2,0,1:T(8,128)(2,1)}, u32[]{:S(2)}, u32[]{:S(2)}) collective-permute-start(bf16[128,2,1024]{2,0,1:T(8,128)(2,1)} %bitcast.147), channel_id=1, source_target_pairs={{0,1},{1,0},{2,3},{3,2},{4,5},{5,4},{6,7},{7,6},{8,9},{9,8},{10,11... | collective-permute-start | bytes 1572872 | tf_op jit(solution)/shard_map/ppermute | solution.py:22
  243.2 4.4 %copy-start.5 = (bf16[128,1024]{0,1:T(8,128)(2,1)S(1)}, bf16[128,1024]{0,1:T(8,128)(2,1)}, u32[]{:S(2)}) copy-start(bf16[128,1024]{0,1:T(8,128)(2,1)} %copy.75) | copy-start | bytes 786436
  260.4 7.7 %collective-permute-start.12 = (bf16[128,2,1024]{2,0,1:T(8,128)(2,1)S(1)}, bf16[128,2,1024]{2,0,1:T(8,128)(2,1)S(1)}, u32[]{:S(2)}, u32[]{:S(2)}) collective-permute-start(bf16[128,2,1024]{2,0,1:T(8,128)(2,1)S(1)} %bitcast.164), channel_id=1, source_target_pairs={{0,1},{1,0},{2,3},{3,2},{4,5},{5,4},{6,7},{7,6},{8,9},{9,8},{10,11... | collective-permute-start | bytes 1572872 | tf_op jit(solution)/shard_map/ppermute | solution.py:22
  265.6 20.2 %collective-permute-start.10 = (bf16[128,1024]{1,0:T(8,128)(2,1)S(1)}, bf16[128,1024]{1,0:T(8,128)(2,1)S(1)}, u32[]{:S(2)}, u32[]{:S(2)}) collective-permute-start(bf16[128,1024]{1,0:T(8,128)(2,1)S(1)} %fusion.34), channel_id=1, source_target_pairs={{0,2},{2,0},{1,3},{3,1},{4,6},{6,4},{5,7},{7,5},{8,10},{10,8},{9,1... | collective-permute-start | bytes 786440 | tf_op jit(solution)/shard_map/ppermute | solution.py:22
  268.5 23.0 %collective-permute-start.13 = (bf16[128,1024]{1,0:T(8,128)(2,1)S(1)}, bf16[128,1024]{1,0:T(8,128)(2,1)S(1)}, u32[]{:S(2)}, u32[]{:S(2)}) collective-permute-start(bf16[128,1024]{1,0:T(8,128)(2,1)S(1)} %fusion.35), channel_id=1, source_target_pairs={{0,2},{2,0},{1,3},{3,1},{4,6},{6,4},{5,7},{7,5},{8,10},{10,8},{9,1... | collective-permute-start | bytes 786440 | tf_op jit(solution)/shard_map/ppermute | solution.py:22

commit v2 on v1

v2 whole, which is shorter than its diff:
```python
import jax
import jax.numpy as jnp
from jax import lax
from jax.sharding import Mesh, PartitionSpec as P

OFF_WEIGHT = 0.0125
EPSILON = 1e-05
F32 = jnp.float32
BF16 = jnp.bfloat16
PLANE = ("y", "x")
SWAP = [(0, 1), (1, 0)]
EXTRA = 16


def dot(left, right, left_dim, right_dim):
    return lax.dot_general(
        left, right, (((left_dim,), (right_dim,)), ((), ())), preferred_element_type=F32
    )


def swap(value, axis):
    return lax.ppermute(value, axis, SWAP)


def gather_zl(value):
    count = lax.axis_size("zl")
    return lax.all_to_all(
        jnp.broadcast_to(value[None], (count,) + value.shape), "zl", 0, 0, tiled=True
    )


def small_gather_zl(value):
    count = lax.axis_size("zl")
    parts = [value]
    for shift in range(1, count):
        parts.append(lax.ppermute(value, "zl", [(i, (i + shift) % count) for i in range(count)]))
    return parts


def combine(means, squares, rows):
    mean = sum(means) / len(means)
    return mean, sum(squares) + rows * sum((m - mean) ** 2 for m in means)


def moments(values):
    rows = values.shape[0]
    wide = values.astype(F32)
    mean = jnp.sum(wide, axis=0) / rows
    square = jnp.sum((wide - mean) ** 2, axis=0)
    parts = small_gather_zl(jnp.stack([mean, square]))
    return combine([p[0] for p in parts], [p[1] for p in parts], rows)


def split(vector, pieces):
    out = []
    for _ in range(pieces):
        high = lax.reduce_precision(vector, 8, 7)
        out.append(high.astype(BF16))
        vector = vector - high
    return out


def extra_rows(vectors):
    rows = [piece for vector, pieces in vectors for piece in split(vector, pieces)]
    stacked = jnp.stack(rows)
    return jnp.pad(stacked, ((0, EXTRA - len(rows)),) + ((0, 0),) * (stacked.ndim - 1))


def read_rows(rows, pieces):
    out, at = [], 0
    for count in pieces:
        out.append(sum(rows[at + k] for k in range(count)))
        at += count
    return out


def local(view_one, view_two, proj_weight):
    rows, width = view_one.shape
    n_zl, n_y, n_x = lax.axis_size("zl"), lax.axis_size("y"), lax.axis_size("x")
    n_plane = n_y * n_x
    total_rows = rows * n_zl * n_plane
    blk_i, blk_j = width // n_x, width // n_y
    core = lax.axis_index("c")
    zh = lax.axis_index("zh")

    crossed = swap(view_two, "zh")
    send_one = view_one.reshape(rows, n_x, blk_i).transpose(1, 0, 2)
    send_one = jnp.broadcast_to(send_one[None], (n_y, n_x, rows, blk_i)).reshape(n_plane, rows, blk_i)
    own_one = lax.all_to_all(send_one, PLANE, 0, 0, tiled=True).reshape(n_plane * rows, blk_i)

    def two_blocks(own, other):
        return jnp.concatenate(
            [own.reshape(own.shape[0], n_y, blk_j), other.reshape(own.shape[0], n_y, blk_j)], axis=2
        ).transpose(1, 0, 2)

    stats_own = jnp.stack(moments(view_two))
    stats_all = two_blocks(stats_own, swap(stats_own, "zh"))
    both = jnp.concatenate(
        [
            two_blocks(view_two, crossed),
            extra_rows([(stats_all[:, 0], 3), (stats_all[:, 1], 3)]).transpose(1, 0, 2),
        ],
        axis=1,
    )
    slot_rows = rows + EXTRA
    both = jnp.broadcast_to(both[:, None], (n_y, n_x, slot_rows, 2 * blk_j))
    both = lax.all_to_all(
        both.reshape(n_plane, slot_rows, 2 * blk_j), PLANE, 0, 0, tiled=True
    )
    plane_two = both[:, :rows].reshape(n_plane * rows, 2 * blk_j)
    group_mean, group_square = read_rows(both[:, rows:].astype(F32).transpose(1, 0, 2), (3, 3))
    mean_two = jnp.mean(group_mean, axis=0)
    square_two = jnp.sum(group_square + rows * n_zl * (group_mean - mean_two) ** 2, axis=0)
    rstd_two = lax.rsqrt(square_two / total_rows + EPSILON)

    plane_one = jnp.concatenate([own_one, swap(own_one, "c")], axis=1)
    mean_one, square_one = moments(plane_one)
    rstd_one = lax.rsqrt(square_one / total_rows + EPSILON)
    norm_one = ((plane_one.astype(F32) - mean_one) * rstd_one).astype(BF16)
    norm_two = ((plane_two.astype(F32) - mean_two) * rstd_two).astype(BF16)

    tile_i, tile_j = norm_one.shape[1], norm_two.shape[1]
    part = dot(norm_one, norm_two, 0, 0).astype(BF16).reshape(n_zl, tile_i // n_zl, tile_j)
    sums = extra_rows(
        [(jnp.sum(norm_one.astype(F32), axis=0), 2), (jnp.sum(norm_two.astype(F32), axis=0), 2)]
    )
    part = jnp.concatenate([part, jnp.broadcast_to(sums[None], (n_zl,) + sums.shape)], axis=1)
    part = jnp.sum(lax.all_to_all(part, "zl", 0, 0, tiled=True).astype(F32), axis=0)
    slice_i = tile_i // n_zl
    mu_one, mu_two = (v / total_rows for v in read_rows(part[slice_i:], (2, 2)))
    corr = part[:slice_i] / total_rows
    on_diag = lax.axis_index("x") == lax.axis_index("y")

    def diagonal(height, first):
        row_ids = first + lax.broadcasted_iota(jnp.int32, (height, tile_j), 0)
        col_ids = lax.broadcasted_iota(jnp.int32, (height, tile_j), 1)
        return (row_ids == col_ids) & (row_ids < blk_i) & on_diag

    grad = jnp.where(
        diagonal(slice_i, lax.axis_index("zl") * slice_i),
        -2.0 * (1.0 - corr),
        2.0 * OFF_WEIGHT * corr,
    ).astype(BF16)
    grad = gather_zl(grad).reshape(tile_i, tile_j)

    wide = grad.astype(F32)
    product = wide * jnp.where(diagonal(tile_i, 0), 1.0 + 0.5 * wide, wide / (2.0 * OFF_WEIGHT))
    cross_one, mean_up_one = jnp.sum(product, axis=1), jnp.sum(wide * mu_two[None, :], axis=1)
    cross_two, mean_up_two = jnp.sum(product, axis=0), jnp.sum(wide * mu_one[:, None], axis=0)

    def to_rows(upstream, vectors):
        columns = upstream.shape[1]
        extra = extra_rows(vectors)
        slots = upstream.astype(BF16).reshape(n_plane, rows, columns)
        return jnp.concatenate([slots, jnp.broadcast_to(extra[None], (n_plane,) + extra.shape)], axis=1)

    def exchange(slots):
        out = lax.all_to_all(slots, PLANE, 0, 0, tiled=True)
        return out.reshape(n_y, n_x, slot_rows, slots.shape[2]).astype(F32)

    def delta(view, upstream, cross, mean_up, mean, rstd):
        normal = ((view.astype(F32) - mean) * rstd).astype(BF16).astype(F32)
        return (rstd * (upstream - mean_up - normal * cross)).astype(BF16)

    pieces = (2, 2, 3, 3)
    slots_two = to_rows(
        dot(norm_one, grad, 1, 0),
        [(cross_two, 2), (mean_up_two, 2), (mean_two / n_x, 3), (rstd_two / n_x, 3)],
    )
    got_two = lax.all_to_all(slots_two, PLANE, 0, 0, tiled=True)

    up_one = dot(norm_two, grad, 1, 1)
    other = jnp.concatenate(
        [
            up_one[:, blk_i:].astype(BF16),
            extra_rows([(cross_one[blk_i:], 2), (mean_up_one[blk_i:], 2)]),
        ],
        axis=0,
    )
    other = swap(other, "c").astype(F32)
    plane_rows = n_plane * rows
    up_one = up_one[:, :blk_i] + other[:plane_rows]
    tail = read_rows(other[plane_rows:], (2, 2))
    slots_one = to_rows(
        up_one,
        [
            (cross_one[:blk_i] + tail[0], 2),
            (mean_up_one[:blk_i] + tail[1], 2),
            (mean_one[:blk_i] / n_y, 3),
            (rstd_one[:blk_i] / n_y, 3),
        ],
    )
    got_two, slots_one = lax.optimization_barrier((got_two, slots_one))
    got_one = lax.all_to_all(slots_one, PLANE, 0, 0, tiled=True)

    got_two = jnp.sum(
        got_two.reshape(n_y, n_x, slot_rows, 2 * blk_j).astype(F32), axis=1
    ).transpose(1, 0, 2)
    own_two, far_two = got_two[:, :, :blk_j].reshape(slot_rows, width), got_two[:, :, blk_j:].reshape(slot_rows, width)
    far_cross, far_mean = read_rows(far_two[rows:], (2, 2))
    sent = jnp.concatenate(
        [far_two[:rows].astype(BF16), extra_rows([(far_cross, 2), (far_mean, 2)])], axis=0
    )
    sent = swap(sent, "zh").astype(F32)
    cross_two, mean_up_two, mean_two, rstd_two = read_rows(own_two[rows:], pieces)
    far_cross, far_mean = read_rows(sent[rows:], (2, 2))
    delta_two = delta(
        view_two, own_two[:rows] + sent[:rows], cross_two + far_cross, mean_up_two + far_mean, mean_two, rstd_two
    )

    got_one = jnp.sum(got_one.reshape(n_y, n_x, slot_rows, blk_i).astype(F32), axis=0)
    got_one = got_one.transpose(1, 0, 2).reshape(slot_rows, width)
    delta_one = delta(view_one, got_one[:rows], *read_rows(got_one[rows:], pieces))

    weight = proj_weight.reshape(2, 2, width, width)

    def block(half, member):
        return lax.dynamic_slice(weight, (half, member, 0, 0), (1, 1, width, width)).reshape(width, width)

    far_give, far_keep = block(1 - zh, 1 - core), block(1 - zh, core)
    near_give, near_keep = block(zh, 1 - core), block(zh, core)

    def input_grad(value):
        far = dot(value, far_keep, 1, 1) + swap(dot(value, far_give, 1, 1).astype(BF16), "c").astype(F32)
        far = swap(far.astype(BF16), "zh").astype(F32)
        near = dot(value, near_keep, 1, 1) + swap(dot(value, near_give, 1, 1).astype(BF16), "c").astype(F32)
        return (near + far).astype(BF16)

    grad_two = input_grad(delta_two)
    return input_grad(delta_one), grad_two


def solution(mesh):
    fine = Mesh(mesh.devices.reshape(4, 4, 4, 2, 2), ("zl", "y", "x", "zh", "c"))
    spec = P(("zl", "y", "x"), ("zh", "c"))
    return jax.shard_map(
        local,
        mesh=fine,
        in_specs=(spec, spec, P(None, ("zh", "c"))),
        out_specs=(spec, spec),
        check_vma=False,
    )
```

time: 295 us -> 266 us (0.902)
  starting transfers between devices: 93.5 us -> 60.6 us
  local copies, waits for them, and re-layouts: 27.7 us -> 12.2 us
  waiting for transfers between devices: 118 us -> 133 us
  matrix products: 22.8 us -> 26.9 us
    ppermute x8 -> x11, starting transfers between devices: 41.1 us -> 24.7 us  [swap(): return lax.ppermute(value, axis, SWAP)]
    ppermute x6, starting transfers between devices: 17.4 us -> 9.6 us  [small_gather_zl(): lax.ppermute(value, 'zl', [(i, (i + shift) % count) for i in range(count)])]
    all_to_all x5 -> x3, starting transfers between devices: 19 us -> 11.4 us  [the longest x1 3.93 us: local(): got_one = lax.all_to_all(slots_one, PLANE, 0, 0, tiled=True)]
    all_to_all x1, waiting for transfers between devices: 2.09 us -> 9.61 us  [local(): lax.all_to_all(send_one, PLANE, 0, 0, tiled=True)]
    reshape x4 -> x3, local copies, waits for them, and re-layouts: 6.42 us -> 0.38 us  [the longest x2 0.2 us: two_blocks(): other.reshape(own.shape[0], n_y, blk_j)]
    unnamed x46 -> x16, local copies, waits for them, and re-layouts: 9.15 us -> 4.78 us
    dynamic_slice x4 -> x0, local copies, waits for them, and re-layouts: 4.32 us -> none  [the longest x2 2.18 us: input_grad(): keep = lax.dynamic_index_in_dim(part, core, 2, keepdims=False)]
    dot_general x5 -> x11, matrix products: 22.8 us -> 26.9 us  [dot(): lax.dot_general(left, right, (((left_dim,), (right_dim,)), ((), ())), pre...]
  transfers between devices with their start and end apart: 22 -> 23, of which waited for: 14 -> 13; matrix products, arithmetic and copies ran while one was open for 19% -> 17% of each run, Pallas kernels for 0% -> 0%
where the time goes in v2:
time: 266 us; the launch traced here: 264 us
  waiting for transfers between devices  133 us (50%)
  starting transfers between devices  60.6 us (23%)
  other arithmetic  30 us (11%)
  matrix products  26.9 us (10%)
  local copies, waits for them, and re-layouts  12.2 us (5%)
    ppermute x11, waiting for transfers between devices, swap(): return lax.ppermute(value, axis, SWAP)  32.1 us
    all_to_all x1, waiting for transfers between devices, local(): got_two = lax.all_to_all(slots_two, PLANE, 0, 0, tiled=True)  31.1 us
    dot_general x11, matrix products, dot(): lax.dot_general(left, right, (((left_dim,), (right_dim,)), ((), ())), pre...  26.9 us
    all_to_all x1, waiting for transfers between devices, local(): lax.all_to_all(both.reshape(n_plane, slot_rows, 2 * blk_j), PLANE, 0, 0,...  26.8 us
    ppermute x11, starting transfers between devices, swap(): return lax.ppermute(value, axis, SWAP)  24.7 us
    all_to_all x1, waiting for transfers between devices, local(): lax.all_to_all(part, 'zl', 0, 0, tiled=True).astype(F32)  15.4 us
    all_to_all x1, waiting for transfers between devices, gather_zl(): lax.all_to_all(jnp.broadcast_to(value[None], (count,) + value.shape), 'zl...  14 us
    all_to_all x1, waiting for transfers between devices, local(): lax.all_to_all(send_one, PLANE, 0, 0, tiled=True)  9.61 us
  transfers between devices with their start and end apart: 23, of which 13 were waited for; matrix products, arithmetic and copies ran while one was open for 17% of the time, Pallas kernels for 0%

profile of v2, /device:TPU:1, one launch (start us, length us, event | category | flops | bytes accessed | tf_op | source)
XLA Modules:
  0.0 264.4 jit_solution(1984799858191181943)
XLA Ops:
  0.6 1.1 copy.61
  2.3 2.5 collective-permute-start.5
  4.9 3.0 %collective-permute-start.6 = (f32[2,1024]{1,0:T(2,128)S(1)}, f32[2,1024]{1,0:T(2,128)S(1)}, u32[]{:S(2)}, u32[]{:S(2)}) collective-permute-start(f32[2,1024]{1,0:T(2,128)S(1)} %pad_maximum_fusion.6), channel_id=1, source_target_pairs={{0,128},{64,192},{128,0},{192,64},{1,129},{65,193},{129,1},{193,65... | collective-permute-start | bytes 24584 | tf_op jit(solution)/shard_map/ppermute | solution.py:36
  8.9 1.8 collective-permute-done.7
  12.6 4.4 %collective-permute-start.8 = (f32[2,1024]{1,0:T(2,128)S(1)}, f32[2,1024]{1,0:T(2,128)S(1)}, u32[]{:S(2)}, u32[]{:S(2)}) collective-permute-start(f32[2,1024]{1,0:T(2,128)S(1)} %pad_maximum_fusion.7), channel_id=1, source_target_pairs={{0,2},{2,0},{1,3},{3,1},{4,6},{6,4},{5,7},{7,5},{8,10},{10,8},{9,1... | collective-permute-start | bytes 24584 | tf_op jit(solution)/shard_map/ppermute | solution.py:22
  17.0 1.0 collective-permute-start.4
  18.0 1.1 reshape.768
  19.2 1.1 broadcast_in_dim.12
  20.3 6.4 %all-to-all-start = ((bf16[16,128,256]{2,1,0:T(8,128)(2,1)}), bf16[16,128,256]{2,1,0:T(8,128)(2,1)S(1)}, u32[]{:S(2)}, u32[]{:S(2)}) async-start(bf16[16,128,256]{2,1,0:T(8,128)(2,1)} %bitcast.1), calls=%async_computation | async-start | bytes 2097152 | tf_op jit(solution)/shard_map/all_to_all | solution.py:89
  27.1 3.6 %collective-permute-done.4 = bf16[128,1024]{1,0:T(8,128)(2,1)S(1)} collective-permute-done((bf16[128,1024]{1,0:T(8,128)(2,1)}, bf16[128,1024]{1,0:T(8,128)(2,1)S(1)}, u32[]{:S(2)}, u32[]{:S(2)}) %collective-permute-start.4) | collective-permute-done | bytes 262176 | tf_op jit(solution)/shard_map/ppermute | solution.py:22
  31.2 9.6 %all-to-all-done = bf16[16,128,256]{2,1,0:T(8,128)(2,1)S(1)} async-done(((bf16[16,128,256]{2,1,0:T(8,128)(2,1)}), bf16[16,128,256]{2,1,0:T(8,128)(2,1)S(1)}, u32[]{:S(2)}, u32[]{:S(2)}) %all-to-all-start) | async-done | bytes 1048608 | tf_op jit(solution)/shard_map/all_to_all | solution.py:89
  40.8 4.5 %collective-permute-start = (bf16[2048,256]{1,0:T(8,128)(2,1)S(1)}, bf16[2048,256]{1,0:T(8,128)(2,1)}, u32[]{:S(2)}, u32[]{:S(2)}) collective-permute-start(bf16[2048,256]{1,0:T(8,128)(2,1)S(1)} %bitcast.172), channel_id=1, source_target_pairs={{0,1},{1,0},{2,3},{3,2},{4,5},{5,4},{6,7},{7,6},{8,9},{9,8},{10,11... | collective-permute-start | bytes 3145736 | tf_op jit(solution)/shard_map/ppermute | solution.py:22
  45.8 1.7 broadcast_in_dim.13
  47.4 3.7 %all-to-all-start.1 = ((bf16[16,144,512]{2,1,0:T(8,128)(2,1)}), bf16[16,144,512]{2,1,0:T(8,128)(2,1)S(1)}, u32[]{:S(2)}, u32[]{:S(2)}) async-start(bf16[16,144,512]{2,1,0:T(8,128)(2,1)} %bitcast.179), calls=%async_computation.1 | async-start | bytes 4718592 | tf_op jit(solution)/shard_map/all_to_all | solution.py:107
  51.2 1.6 convert_reduce_fusion
  52.7 1.8 fusion.1
  54.6 0.9 collective-permute-start.1
  55.5 2.0 collective-permute-start.2
  57.9 1.3 collective-permute-done.1
  59.2 1.0 collective-permute-done.3
  60.3 1.8 convert_reduce_fusion.3
  62.1 26.8 %all-to-all-done.1 = bf16[16,144,512]{2,1,0:T(8,128)(2,1)S(1)} async-done(((bf16[16,144,512]{2,1,0:T(8,128)(2,1)}), bf16[16,144,512]{2,1,0:T(8,128)(2,1)S(1)}, u32[]{:S(2)}, u32[]{:S(2)}) %all-to-all-start.1) | async-done | bytes 2359328 | tf_op jit(solution)/shard_map/all_to_all | solution.py:107
  90.4 2.1 convert_reduce_fusion.2
  92.5 2.5 convolution_convert_fusion.1
  95.0 0.9 pad_maximum_fusion.5
  95.9 4.3 %all-to-all-start.2 = ((bf16[4,144,512]{2,1,0:T(8,128)(2,1)}), bf16[4,144,512]{2,1,0:T(8,128)(2,1)}, u32[]{:S(2)}, u32[]{:S(2)}) async-start(bf16[4,144,512]{2,1,0:T(8,128)(2,1)} %pad_maximum_fusion.5), calls=%async_computation.2 | async-start | bytes 1179648 | tf_op jit(solution)/shard_map/all_to_all | solution.py:128
  100.2 15.4 %all-to-all-done.2 = bf16[4,144,512]{2,1,0:T(8,128)(2,1)} async-done(((bf16[4,144,512]{2,1,0:T(8,128)(2,1)}), bf16[4,144,512]{2,1,0:T(8,128)(2,1)}, u32[]{:S(2)}, u32[]{:S(2)}) %all-to-all-start.2) | async-done | bytes 589856 | tf_op jit(solution)/shard_map/all_to_all | solution.py:128
  115.6 1.2 convert_reduce_fusion.5
  117.0 0.8 broadcast_in_dim.15
  117.8 4.1 %all-to-all-start.3 = ((bf16[4,128,512]{2,1,0:T(8,128)(2,1)}), bf16[4,128,512]{2,1,0:T(8,128)(2,1)}, u32[]{:S(2)}, u32[]{:S(2)}) async-start(bf16[4,128,512]{2,1,0:T(8,128)(2,1)} %broadcast_in_dim.15), calls=%async_computation.3 | async-start | bytes 1048576 | tf_op jit(solution)/shard_map/all_to_all | solution.py:27
  122.0 14.0 %all-to-all-done.3 = bf16[4,128,512]{2,1,0:T(8,128)(2,1)} async-done(((bf16[4,128,512]{2,1,0:T(8,128)(2,1)}), bf16[4,128,512]{2,1,0:T(8,128)(2,1)}, u32[]{:S(2)}, u32[]{:S(2)}) %all-to-all-start.3) | async-done | bytes 524320 | tf_op jit(solution)/shard_map/all_to_all | solution.py:27
  136.0 2.4 fusion.147
  138.6 2.3 fusion.52
  141.0 1.0 pad_maximum_fusion.3
  142.0 1.5 collective-permute-start.9
  143.5 2.6 convolution_convert_fusion
  146.2 1.6 pad_maximum_fusion
  147.9 3.7 %all-to-all-start.4 = ((bf16[16,144,512]{2,1,0:T(8,128)(2,1)}), bf16[16,144,512]{2,1,0:T(8,128)(2,1)S(1)}, u32[]{:S(2)}, u32[]{:S(2)}) async-start(bf16[16,144,512]{2,1,0:T(8,128)(2,1)} %pad_maximum_fusion), calls=%async_computation.4 | async-start | bytes 4718592 | tf_op jit(solution)/shard_map/all_to_all | solution.py:170
  151.7 1.4 convert_element_type.504
  153.1 1.4 copy-done.2
  154.6 2.4 fusion.6
  157.1 1.1 pad_maximum_fusion.2
  158.2 31.1 %all-to-all-done.4 = bf16[16,144,512]{2,1,0:T(8,128)(2,1)S(1)} async-done(((bf16[16,144,512]{2,1,0:T(8,128)(2,1)}), bf16[16,144,512]{2,1,0:T(8,128)(2,1)S(1)}, u32[]{:S(2)}, u32[]{:S(2)}) %all-to-all-start.4) | async-done | bytes 2359328 | tf_op jit(solution)/shard_map/all_to_all | solution.py:170
  190.1 0.9 fusion.58
  191.1 4.8 %collective-permute-start.13 = (bf16[144,1024]{0,1:T(8,128)(2,1)}, bf16[144,1024]{0,1:T(8,128)(2,1)}, u32[]{:S(2)}, u32[]{:S(2)}) collective-permute-start(bf16[144,1024]{0,1:T(8,128)(2,1)} %fusion.58), channel_id=1, source_target_pairs={{0,2},{2,0},{1,3},{3,1},{4,6},{6,4},{5,7},{7,5},{8,10},{10,8},{9,1... | collective-permute-start | bytes 884744 | tf_op jit(solution)/shard_map/ppermute | solution.py:22
  195.8 1.8 copy.67
  198.3 3.9 %all-to-all-start.5 = ((bf16[16,144,256]{2,1,0:T(8,128)(2,1)}), bf16[16,144,256]{2,1,0:T(8,128)(2,1)S(1)}, u32[]{:S(2)}, u32[]{:S(2)}) async-start(bf16[16,144,256]{2,1,0:T(8,128)(2,1)} %pad_maximum_fusion.2), calls=%async_computation.5 | async-start | bytes 2359296 | tf_op jit(solution)/shard_map/all_to_all | solution.py:194
  202.3 16.9 %collective-permute-done.13 = bf16[144,1024]{0,1:T(8,128)(2,1)} collective-permute-done((bf16[144,1024]{0,1:T(8,128)(2,1)}, bf16[144,1024]{0,1:T(8,128)(2,1)}, u32[]{:S(2)}, u32[]{:S(2)}) %collective-permute-start.13) | collective-permute-done | bytes 294944 | tf_op jit(solution)/shard_map/ppermute | solution.py:22
  219.2 1.1 convert_element_type.536
  221.7 2.4 fusion.40
  224.2 1.9 collective-permute-start.15
  226.1 2.4 fusion.34
  228.6 2.4 fusion.19
  232.6 2.4 fusion.37
  235.6 2.4 add_convert_fusion.1
  238.0 2.5 collective-permute-start.16
  240.5 2.4 fusion.31
  243.3 2.4 add_convert_fusion.3
  245.7 3.1 %collective-permute-start.12 = (bf16[128,1024]{1,0:T(8,128)(2,1)S(1)}, bf16[128,1024]{1,0:T(8,128)(2,1)S(1)}, u32[]{:S(2)}, u32[]{:S(2)}) collective-permute-start(bf16[128,1024]{1,0:T(8,128)(2,1)S(1)} %add_convert_fusion.3), channel_id=1, source_target_pairs={{0,2},{2,0},{1,3},{3,1},{4,6},{6,4},{5,7},{7,5},{8,10},{10,8},{9,1... | collective-permute-start | bytes 786440 | tf_op jit(solution)/shard_map/ppermute | solution.py:22
  248.8 4.0 %collective-permute-done.16 = bf16[128,1024]{1,0:T(8,128)(2,1)S(1)} collective-permute-done((bf16[128,1024]{1,0:T(8,128)(2,1)S(1)}, bf16[128,1024]{1,0:T(8,128)(2,1)S(1)}, u32[]{:S(2)}, u32[]{:S(2)}) %collective-permute-start.16) | collective-permute-done | bytes 262176 | tf_op jit(solution)/shard_map/ppermute | solution.py:22
  252.8 0.8 add_convert_fusion
  253.6 2.4 fusion.21
  256.1 7.5 %collective-permute-done.12 = bf16[128,1024]{1,0:T(8,128)(2,1)S(1)} collective-permute-done((bf16[128,1024]{1,0:T(8,128)(2,1)S(1)}, bf16[128,1024]{1,0:T(8,128)(2,1)S(1)}, u32[]{:S(2)}, u32[]{:S(2)}) %collective-permute-start.12) | collective-permute-done | bytes 262176 | tf_op jit(solution)/shard_map/ppermute | solution.py:22
  263.6 0.8 add_convert_fusion.2
  (119 shorter events, 12.9 us)
Async XLA Ops:
  1.8 18.5 %copy-start.3 = (bf16[128,1024]{0,1:T(8,128)(2,1)}, bf16[128,1024]{0,1:T(8,128)(2,1)S(1)}, u32[]{:S(2)}) copy-start(bf16[128,1024]{0,1:T(8,128)(2,1)S(1)} %copy.61) | copy-start | bytes 786436
  1.9 24.8 %copy-start.5 = (bf16[128,1024]{1,0:T(8,128)(2,1)S(1)}, bf16[128,1024]{1,0:T(8,128)(2,1)}, u32[]{:S(2)}) copy-start(bf16[128,1024]{1,0:T(8,128)(2,1)} %param.4) | copy-start | bytes 786436
  2.3 6.3 %collective-permute-start.5 = (f32[2,1024]{1,0:T(2,128)S(1)}, f32[2,1024]{1,0:T(2,128)S(1)}, u32[]{:S(2)}, u32[]{:S(2)}) collective-permute-start(f32[2,1024]{1,0:T(2,128)S(1)} %pad_maximum_fusion.6), channel_id=1, source_target_pairs={{0,64},{64,128},{128,192},{192,0},{1,65},{65,129},{129,193},{193,1... | collective-permute-start | bytes 24584 | tf_op jit(solution)/shard_map/ppermute | solution.py:36
  4.9 4.0 %collective-permute-start.6 = (f32[2,1024]{1,0:T(2,128)S(1)}, f32[2,1024]{1,0:T(2,128)S(1)}, u32[]{:S(2)}, u32[]{:S(2)}) collective-permute-start(f32[2,1024]{1,0:T(2,128)S(1)} %pad_maximum_fusion.6), channel_id=1, source_target_pairs={{0,128},{64,192},{128,0},{192,64},{1,129},{65,193},{129,1},{193,65... | collective-permute-start | bytes 24584 | tf_op jit(solution)/shard_map/ppermute | solution.py:36
  7.9 2.8 %collective-permute-start.7 = (f32[2,1024]{1,0:T(2,128)S(1)}, f32[2,1024]{1,0:T(2,128)S(1)}, u32[]{:S(2)}, u32[]{:S(2)}) collective-permute-start(f32[2,1024]{1,0:T(2,128)S(1)} %pad_maximum_fusion.6), channel_id=1, source_target_pairs={{0,192},{64,0},{128,64},{192,128},{1,193},{65,1},{129,65},{193,129... | collective-permute-start | bytes 24584 | tf_op jit(solution)/shard_map/ppermute | solution.py:36
  12.6 14.4 %collective-permute-start.8 = (f32[2,1024]{1,0:T(2,128)S(1)}, f32[2,1024]{1,0:T(2,128)S(1)}, u32[]{:S(2)}, u32[]{:S(2)}) collective-permute-start(f32[2,1024]{1,0:T(2,128)S(1)} %pad_maximum_fusion.7), channel_id=1, source_target_pairs={{0,2},{2,0},{1,3},{3,1},{4,6},{6,4},{5,7},{7,5},{8,10},{10,8},{9,1... | collective-permute-start | bytes 24584 | tf_op jit(solution)/shard_map/ppermute | solution.py:22
  17.0 13.8 %collective-permute-start.4 = (bf16[128,1024]{1,0:T(8,128)(2,1)}, bf16[128,1024]{1,0:T(8,128)(2,1)S(1)}, u32[]{:S(2)}, u32[]{:S(2)}) collective-permute-start(bf16[128,1024]{1,0:T(8,128)(2,1)} %param.4), channel_id=1, source_target_pairs={{0,2},{2,0},{1,3},{3,1},{4,6},{6,4},{5,7},{7,5},{8,10},{10,8},{9,1... | collective-permute-start | bytes 786440 | tf_op jit(solution)/shard_map/ppermute | solution.py:22
  20.3 20.5 %all-to-all-start = ((bf16[16,128,256]{2,1,0:T(8,128)(2,1)}), bf16[16,128,256]{2,1,0:T(8,128)(2,1)S(1)}, u32[]{:S(2)}, u32[]{:S(2)}) async-start(bf16[16,128,256]{2,1,0:T(8,128)(2,1)} %bitcast.1), calls=%async_computation | async-start | bytes 2097152 | tf_op jit(solution)/shard_map/all_to_all | solution.py:89
  40.8 10.4 %collective-permute-start = (bf16[2048,256]{1,0:T(8,128)(2,1)S(1)}, bf16[2048,256]{1,0:T(8,128)(2,1)}, u32[]{:S(2)}, u32[]{:S(2)}) collective-permute-start(bf16[2048,256]{1,0:T(8,128)(2,1)S(1)} %bitcast.172), channel_id=1, source_target_pairs={{0,1},{1,0},{2,3},{3,2},{4,5},{5,4},{6,7},{7,6},{8,9},{9,8},{10,11... | collective-permute-start | bytes 3145736 | tf_op jit(solution)/shard_map/ppermute | solution.py:22
  47.4 41.5 %all-to-all-start.1 = ((bf16[16,144,512]{2,1,0:T(8,128)(2,1)}), bf16[16,144,512]{2,1,0:T(8,128)(2,1)S(1)}, u32[]{:S(2)}, u32[]{:S(2)}) async-start(bf16[16,144,512]{2,1,0:T(8,128)(2,1)} %bitcast.179), calls=%async_computation.1 | async-start | bytes 4718592 | tf_op jit(solution)/shard_map/all_to_all | solution.py:107
  54.6 4.6 %collective-permute-start.1 = (f32[2,512]{1,0:T(2,128)S(1)}, f32[2,512]{1,0:T(2,128)S(1)}, u32[]{:S(2)}, u32[]{:S(2)}) collective-permute-start(f32[2,512]{1,0:T(2,128)S(1)} %pad_maximum_fusion.9), channel_id=1, source_target_pairs={{0,64},{64,128},{128,192},{192,0},{1,65},{65,129},{129,193},{193,1... | collective-permute-start | bytes 12296 | tf_op jit(solution)/shard_map/ppermute | solution.py:36
  55.5 3.7 %collective-permute-start.2 = (f32[2,512]{1,0:T(2,128)S(1)}, f32[2,512]{1,0:T(2,128)S(1)}, u32[]{:S(2)}, u32[]{:S(2)}) collective-permute-start(f32[2,512]{1,0:T(2,128)S(1)} %pad_maximum_fusion.9), channel_id=1, source_target_pairs={{0,128},{64,192},{128,0},{192,64},{1,129},{65,193},{129,1},{193,65... | collective-permute-start | bytes 12296 | tf_op jit(solution)/shard_map/ppermute | solution.py:36
  57.5 2.8 %collective-permute-start.3 = (f32[2,512]{1,0:T(2,128)S(1)}, f32[2,512]{1,0:T(2,128)S(1)}, u32[]{:S(2)}, u32[]{:S(2)}) collective-permute-start(f32[2,512]{1,0:T(2,128)S(1)} %pad_maximum_fusion.9), channel_id=1, source_target_pairs={{0,192},{64,0},{128,64},{192,128},{1,193},{65,1},{129,65},{193,129... | collective-permute-start | bytes 12296 | tf_op jit(solution)/shard_map/ppermute | solution.py:36
  95.9 40.1 %copy-start.1 = (bf16[16,128,512]{2,1,0:T(8,128)(2,1)S(1)}, bf16[16,128,512]{2,1,0:T(8,128)(2,1)}, u32[]{:S(2)}) copy-start(bf16[16,128,512]{2,1,0:T(8,128)(2,1)} %get-tuple-element.19) | copy-start | bytes 6291460
  95.9 19.8 %all-to-all-start.2 = ((bf16[4,144,512]{2,1,0:T(8,128)(2,1)}), bf16[4,144,512]{2,1,0:T(8,128)(2,1)}, u32[]{:S(2)}, u32[]{:S(2)}) async-start(bf16[4,144,512]{2,1,0:T(8,128)(2,1)} %pad_maximum_fusion.5), calls=%async_computation.2 | async-start | bytes 1179648 | tf_op jit(solution)/shard_map/all_to_all | solution.py:128
  117.8 18.2 %all-to-all-start.3 = ((bf16[4,128,512]{2,1,0:T(8,128)(2,1)}), bf16[4,128,512]{2,1,0:T(8,128)(2,1)}, u32[]{:S(2)}, u32[]{:S(2)}) async-start(bf16[4,128,512]{2,1,0:T(8,128)(2,1)} %broadcast_in_dim.15), calls=%async_computation.3 | async-start | bytes 1048576 | tf_op jit(solution)/shard_map/all_to_all | solution.py:27
  138.4 3.6 %copy-start = (f32[2048,512]{1,0:T(8,128)}, f32[2048,512]{1,0:T(8,128)S(1)}, u32[]{:S(2)}) copy-start(f32[2048,512]{1,0:T(8,128)S(1)} %fusion.147) | copy-start | bytes 12582916
  142.0 9.7 %collective-permute-start.9 = (bf16[2064,256]{1,0:T(8,128)(2,1)}, bf16[2064,256]{1,0:T(8,128)(2,1)}, u32[]{:S(2)}, u32[]{:S(2)}) collective-permute-start(bf16[2064,256]{1,0:T(8,128)(2,1)} %pad_maximum_fusion.3), channel_id=1, source_target_pairs={{0,1},{1,0},{2,3},{3,2},{4,5},{5,4},{6,7},{7,6},{8,9},{9,8},{10,11... | collective-permute-start | bytes 3170312 | tf_op jit(solution)/shard_map/ppermute | solution.py:22
  147.9 41.3 %all-to-all-start.4 = ((bf16[16,144,512]{2,1,0:T(8,128)(2,1)}), bf16[16,144,512]{2,1,0:T(8,128)(2,1)S(1)}, u32[]{:S(2)}, u32[]{:S(2)}) async-start(bf16[16,144,512]{2,1,0:T(8,128)(2,1)} %pad_maximum_fusion), calls=%async_computation.4 | async-start | bytes 4718592 | tf_op jit(solution)/shard_map/all_to_all | solution.py:170
  153.1 1.4 copy-start.2
  191.1 28.1 %collective-permute-start.13 = (bf16[144,1024]{0,1:T(8,128)(2,1)}, bf16[144,1024]{0,1:T(8,128)(2,1)}, u32[]{:S(2)}, u32[]{:S(2)}) collective-permute-start(bf16[144,1024]{0,1:T(8,128)(2,1)} %fusion.58), channel_id=1, source_target_pairs={{0,2},{2,0},{1,3},{3,1},{4,6},{6,4},{5,7},{7,5},{8,10},{10,8},{9,1... | collective-permute-start | bytes 884744 | tf_op jit(solution)/shard_map/ppermute | solution.py:22
  198.3 32.7 %all-to-all-start.5 = ((bf16[16,144,256]{2,1,0:T(8,128)(2,1)}), bf16[16,144,256]{2,1,0:T(8,128)(2,1)S(1)}, u32[]{:S(2)}, u32[]{:S(2)}) async-start(bf16[16,144,256]{2,1,0:T(8,128)(2,1)} %pad_maximum_fusion.2), calls=%async_computation.5 | async-start | bytes 2359296 | tf_op jit(solution)/shard_map/all_to_all | solution.py:194
  202.3 18.8 %copy-start.4 = (bf16[128,1024]{0,1:T(8,128)(2,1)S(1)}, bf16[128,1024]{0,1:T(8,128)(2,1)}, u32[]{:S(2)}) copy-start(bf16[128,1024]{0,1:T(8,128)(2,1)} %copy-done.3) | copy-start | bytes 786436
  224.2 11.4 %collective-permute-start.15 = (bf16[128,1024]{1,0:T(8,128)(2,1)S(1)}, bf16[128,1024]{1,0:T(8,128)(2,1)S(1)}, u32[]{:S(2)}, u32[]{:S(2)}) collective-permute-start(bf16[128,1024]{1,0:T(8,128)(2,1)S(1)} %fusion.40), channel_id=1, source_target_pairs={{0,1},{1,0},{2,3},{3,2},{4,5},{5,4},{6,7},{7,6},{8,9},{9,8},{10,11... | collective-permute-start | bytes 786440 | tf_op jit(solution)/shard_map/ppermute | solution.py:22
  228.5 20.3 %collective-permute-start.14 = (bf16[128,1024]{1,0:T(8,128)(2,1)S(1)}, bf16[128,1024]{1,0:T(8,128)(2,1)S(1)}, u32[]{:S(2)}, u32[]{:S(2)}) collective-permute-start(bf16[128,1024]{1,0:T(8,128)(2,1)S(1)} %fusion.34), channel_id=1, source_target_pairs={{0,1},{1,0},{2,3},{3,2},{4,5},{5,4},{6,7},{7,6},{8,9},{9,8},{10,11... | collective-permute-start | bytes 786440 | tf_op jit(solution)/shard_map/ppermute | solution.py:22
  231.0 1.0 copy-start.6
  235.0 8.3 %collective-permute-start.11 = (bf16[128,1024]{1,0:T(8,128)(2,1)S(1)}, bf16[128,1024]{1,0:T(8,128)(2,1)S(1)}, u32[]{:S(2)}, u32[]{:S(2)}) collective-permute-start(bf16[128,1024]{1,0:T(8,128)(2,1)S(1)} %fusion.37), channel_id=1, source_target_pairs={{0,1},{1,0},{2,3},{3,2},{4,5},{5,4},{6,7},{7,6},{8,9},{9,8},{10,11... | collective-permute-start | bytes 786440 | tf_op jit(solution)/shard_map/ppermute | solution.py:22
  238.0 14.8 %collective-permute-start.16 = (bf16[128,1024]{1,0:T(8,128)(2,1)S(1)}, bf16[128,1024]{1,0:T(8,128)(2,1)S(1)}, u32[]{:S(2)}, u32[]{:S(2)}) collective-permute-start(bf16[128,1024]{1,0:T(8,128)(2,1)S(1)} %add_convert_fusion.1), channel_id=1, source_target_pairs={{0,2},{2,0},{1,3},{3,1},{4,6},{6,4},{5,7},{7,5},{8,10},{10,8},{9,1... | collective-permute-start | bytes 786440 | tf_op jit(solution)/shard_map/ppermute | solution.py:22
  242.9 13.2 %collective-permute-start.10 = (bf16[128,1024]{1,0:T(8,128)(2,1)S(1)}, bf16[128,1024]{1,0:T(8,128)(2,1)S(1)}, u32[]{:S(2)}, u32[]{:S(2)}) collective-permute-start(bf16[128,1024]{1,0:T(8,128)(2,1)S(1)} %fusion.31), channel_id=1, source_target_pairs={{0,1},{1,0},{2,3},{3,2},{4,5},{5,4},{6,7},{7,6},{8,9},{9,8},{10,11... | collective-permute-start | bytes 786440 | tf_op jit(solution)/shard_map/ppermute | solution.py:22
  245.7 17.9 %collective-permute-start.12 = (bf16[128,1024]{1,0:T(8,128)(2,1)S(1)}, bf16[128,1024]{1,0:T(8,128)(2,1)S(1)}, u32[]{:S(2)}, u32[]{:S(2)}) collective-permute-start(bf16[128,1024]{1,0:T(8,128)(2,1)S(1)} %add_convert_fusion.3), channel_id=1, source_target_pairs={{0,2},{2,0},{1,3},{3,1},{4,6},{6,4},{5,7},{7,5},{8,10},{10,8},{9,1... | collective-permute-start | bytes 786440 | tf_op jit(solution)/shard_map/ppermute | solution.py:22

commit v3 on v2

--- a/solution.py
+++ b/solution.py
@@ -83,47 +83,44 @@
     core = lax.axis_index("c")
     zh = lax.axis_index("zh")
 
+    def column_blocks(view, count):
+        return view.reshape(rows, count, width // count).transpose(1, 0, 2)
+
+    def to_plane(slots):
+        slots = jnp.broadcast_to(slots, (n_y, n_x) + slots.shape[2:])
+        out = lax.all_to_all(slots.reshape((n_plane,) + slots.shape[2:]), PLANE, 0, 0, tiled=True)
+        return out.reshape(n_plane * rows, slots.shape[3])
+
     crossed = swap(view_two, "zh")
-    send_one = view_one.reshape(rows, n_x, blk_i).transpose(1, 0, 2)
-    send_one = jnp.broadcast_to(send_one[None], (n_y, n_x, rows, blk_i)).reshape(n_plane, rows, blk_i)
-    own_one = lax.all_to_all(send_one, PLANE, 0, 0, tiled=True).reshape(n_plane * rows, blk_i)
-
-    def two_blocks(own, other):
-        return jnp.concatenate(
-            [own.reshape(own.shape[0], n_y, blk_j), other.reshape(own.shape[0], n_y, blk_j)], axis=2
-        ).transpose(1, 0, 2)
-
-    stats_own = jnp.stack(moments(view_two))
-    stats_all = two_blocks(stats_own, swap(stats_own, "zh"))
-    both = jnp.concatenate(
-        [
-            two_blocks(view_two, crossed),
-            extra_rows([(stats_all[:, 0], 3), (stats_all[:, 1], 3)]).transpose(1, 0, 2),
-        ],
-        axis=1,
-    )
-    slot_rows = rows + EXTRA
-    both = jnp.broadcast_to(both[:, None], (n_y, n_x, slot_rows, 2 * blk_j))
-    both = lax.all_to_all(
-        both.reshape(n_plane, slot_rows, 2 * blk_j), PLANE, 0, 0, tiled=True
-    )
-    plane_two = both[:, :rows].reshape(n_plane * rows, 2 * blk_j)
-    group_mean, group_square = read_rows(both[:, rows:].astype(F32).transpose(1, 0, 2), (3, 3))
-    mean_two = jnp.mean(group_mean, axis=0)
-    square_two = jnp.sum(group_square + rows * n_zl * (group_mean - mean_two) ** 2, axis=0)
-    rstd_two = lax.rsqrt(square_two / total_rows + EPSILON)
-
-    plane_one = jnp.concatenate([own_one, swap(own_one, "c")], axis=1)
-    mean_one, square_one = moments(plane_one)
-    rstd_one = lax.rsqrt(square_one / total_rows + EPSILON)
-    norm_one = ((plane_one.astype(F32) - mean_one) * rstd_one).astype(BF16)
-    norm_two = ((plane_two.astype(F32) - mean_two) * rstd_two).astype(BF16)
+    own = to_plane(
+        jnp.concatenate(
+            [
+                jnp.broadcast_to(column_blocks(view_one, n_x)[None], (n_y, n_x, rows, blk_i)),
+                jnp.broadcast_to(column_blocks(view_two, n_y)[:, None], (n_y, n_x, rows, blk_j)),
+            ],
+            axis=3,
+        )
+    )
+    crossed, own = lax.optimization_barrier((crossed, own))
+    far_two = to_plane(column_blocks(crossed, n_y)[:, None])
+
+    def normalize(values, mean, rstd):
+        return ((values.astype(F32) - mean) * rstd).astype(BF16)
+
+    mean, square = moments(own)
+    rstd = lax.rsqrt(square / total_rows + EPSILON)
+    far_stats = swap(jnp.stack([mean[blk_i:], rstd[blk_i:]]), "zh")
+    norm_own = normalize(own, mean, rstd)
+    sums_own = jnp.sum(norm_own.astype(F32), axis=0)
+    sums_one = jnp.concatenate([sums_own[:blk_i], swap(sums_own[:blk_i], "c")])
+    sums_two = jnp.concatenate([sums_own[blk_i:], swap(sums_own[blk_i:], "zh")])
+    norm_one = jnp.concatenate([norm_own[:, :blk_i], swap(norm_own[:, :blk_i], "c")], axis=1)
+    norm_two = jnp.concatenate([norm_own[:, blk_i:], normalize(far_two, far_stats[0], far_stats[1])], axis=1)
+    mean_one, rstd_one, mean_two, rstd_two = mean[:blk_i], rstd[:blk_i], mean[blk_i:], rstd[blk_i:]
 
     tile_i, tile_j = norm_one.shape[1], norm_two.shape[1]
     part = dot(norm_one, norm_two, 0, 0).astype(BF16).reshape(n_zl, tile_i // n_zl, tile_j)
-    sums = extra_rows(
-        [(jnp.sum(norm_one.astype(F32), axis=0), 2), (jnp.sum(norm_two.astype(F32), axis=0), 2)]
-    )
+    sums = extra_rows([(sums_one, 2), (sums_two, 2)])
     part = jnp.concatenate([part, jnp.broadcast_to(sums[None], (n_zl,) + sums.shape)], axis=1)
     part = jnp.sum(lax.all_to_all(part, "zl", 0, 0, tiled=True).astype(F32), axis=0)
     slice_i = tile_i // n_zl
@@ -143,10 +140,9 @@
     ).astype(BF16)
     grad = gather_zl(grad).reshape(tile_i, tile_j)
 
-    wide = grad.astype(F32)
-    product = wide * jnp.where(diagonal(tile_i, 0), 1.0 + 0.5 * wide, wide / (2.0 * OFF_WEIGHT))
-    cross_one, mean_up_one = jnp.sum(product, axis=1), jnp.sum(wide * mu_two[None, :], axis=1)
-    cross_two, mean_up_two = jnp.sum(product, axis=0), jnp.sum(wide * mu_one[:, None], axis=0)
+    def products(grad):
+        wide = grad.astype(F32)
+        return wide, wide * jnp.where(diagonal(tile_i, 0), 1.0 + 0.5 * wide, wide / (2.0 * OFF_WEIGHT))
 
     def to_rows(upstream, vectors):
         columns = upstream.shape[1]
@@ -154,21 +150,27 @@
         slots = upstream.astype(BF16).reshape(n_plane, rows, columns)
         return jnp.concatenate([slots, jnp.broadcast_to(extra[None], (n_plane,) + extra.shape)], axis=1)
 
-    def exchange(slots):
-        out = lax.all_to_all(slots, PLANE, 0, 0, tiled=True)
-        return out.reshape(n_y, n_x, slot_rows, slots.shape[2]).astype(F32)
-
     def delta(view, upstream, cross, mean_up, mean, rstd):
         normal = ((view.astype(F32) - mean) * rstd).astype(BF16).astype(F32)
         return (rstd * (upstream - mean_up - normal * cross)).astype(BF16)
 
     pieces = (2, 2, 3, 3)
+    slot_rows = rows + EXTRA
+    wide, product = products(grad)
     slots_two = to_rows(
         dot(norm_one, grad, 1, 0),
-        [(cross_two, 2), (mean_up_two, 2), (mean_two / n_x, 3), (rstd_two / n_x, 3)],
-    )
+        [
+            (jnp.sum(product, axis=0), 2),
+            (jnp.sum(wide * mu_one[:, None], axis=0), 2),
+            (jnp.pad(mean_two, (0, blk_j)) / n_x, 3),
+            (jnp.pad(rstd_two, (0, blk_j)) / n_x, 3),
+        ],
+    )
+    slots_two, grad = lax.optimization_barrier((slots_two, grad))
     got_two = lax.all_to_all(slots_two, PLANE, 0, 0, tiled=True)
 
+    wide, product = products(grad)
+    cross_one, mean_up_one = jnp.sum(product, axis=1), jnp.sum(wide * mu_two[None, :], axis=1)
     up_one = dot(norm_two, grad, 1, 1)
     other = jnp.concatenate(
         [
@@ -186,8 +188,8 @@
         [
             (cross_one[:blk_i] + tail[0], 2),
             (mean_up_one[:blk_i] + tail[1], 2),
-            (mean_one[:blk_i] / n_y, 3),
-            (rstd_one[:blk_i] / n_y, 3),
+            (mean_one / n_y, 3),
+            (rstd_one / n_y, 3),
         ],
     )
     got_two, slots_one = lax.optimization_barrier((got_two, slots_one))

time: 266 us -> 239 us (0.90)
  waiting for transfers between devices: 133 us -> 118 us
  other arithmetic: 30 us -> 18.9 us
    all_to_all x2, waiting for transfers between devices: 36.4 us -> 16.8 us  [to_plane(): lax.all_to_all(slots.reshape((n_plane,) + slots.shape[2:]), PLANE, 0, 0,...]
    ppermute x11 -> x13, waiting for transfers between devices: 32.1 us -> 41.5 us  [swap(): return lax.ppermute(value, axis, SWAP)]
    ppermute x6 -> x3, waiting for transfers between devices: 4.37 us -> 0.01 us  [small_gather_zl(): lax.ppermute(value, 'zl', [(i, (i + shift) % count) for i in range(count)])]
    ppermute x6 -> x3, starting transfers between devices: 9.6 us -> 5.43 us  [small_gather_zl(): lax.ppermute(value, 'zl', [(i, (i + shift) % count) for i in range(count)])]
    all_to_all x1, starting transfers between devices: 3.72 us -> 6.89 us  [local(): got_two = lax.all_to_all(slots_two, PLANE, 0, 0, tiled=True)]
    ppermute x11 -> x13, starting transfers between devices: 24.7 us -> 25.8 us  [swap(): return lax.ppermute(value, axis, SWAP)]
  transfers between devices with their start and end apart: 23 -> 22, of which waited for: 13 -> 9; matrix products, arithmetic and copies ran while one was open for 17% -> 15% of each run, Pallas kernels for 0% -> 0%
where the time goes in v3:
time: 239 us; the launch traced here: 238 us
  waiting for transfers between devices  118 us (49%)
  starting transfers between devices  61.1 us (26%)
  matrix products  26.3 us (11%)
  other arithmetic  18.9 us (8%)
  local copies, waits for them, and re-layouts  12.4 us (5%)
    ppermute x13, waiting for transfers between devices, swap(): return lax.ppermute(value, axis, SWAP)  41.5 us
    all_to_all x1, waiting for transfers between devices, local(): got_two = lax.all_to_all(slots_two, PLANE, 0, 0, tiled=True)  30.4 us
    dot_general x11, matrix products, dot(): lax.dot_general(left, right, (((left_dim,), (right_dim,)), ((), ())), pre...  26.3 us
    ppermute x13, starting transfers between devices, swap(): return lax.ppermute(value, axis, SWAP)  25.8 us
    all_to_all x2, waiting for transfers between devices, to_plane(): lax.all_to_all(slots.reshape((n_plane,) + slots.shape[2:]), PLANE, 0, 0,...  16.8 us
    all_to_all x1, waiting for transfers between devices, local(): lax.all_to_all(part, 'zl', 0, 0, tiled=True).astype(F32)  15.3 us
    all_to_all x1, waiting for transfers between devices, gather_zl(): lax.all_to_all(jnp.broadcast_to(value[None], (count,) + value.shape), 'zl...  13.6 us
    all_to_all x2, starting transfers between devices, to_plane(): lax.all_to_all(slots.reshape((n_plane,) + slots.shape[2:]), PLANE, 0, 0,...  12 us
  transfers between devices with their start and end apart: 22, of which 9 were waited for; matrix products, arithmetic and copies ran while one was open for 15% of the time, Pallas kernels for 0%

profile of v3, /device:TPU:1, one launch (start us, length us, event | category | flops | bytes accessed | tf_op | source)
XLA Modules:
  0.0 237.6 jit_solution(5172001753713320593)
XLA Ops:
  0.6 1.1 reshape.564
  1.8 1.1 reshape.565
  3.2 1.5 pad_maximum_fusion.1
  4.7 7.7 %all-to-all-start = ((bf16[16,128,512]{2,1,0:T(8,128)(2,1)}), bf16[16,128,512]{2,1,0:T(8,128)(2,1)S(1)}, u32[]{:S(2)}, u32[]{:S(2)}) async-start(bf16[16,128,512]{2,1,0:T(8,128)(2,1)} %bitcast.119), calls=%async_computation | async-start | bytes 4194304 | tf_op jit(solution)/shard_map/all_to_all | solution.py:91
  12.5 7.0 %collective-permute-start = (bf16[128,1024]{1,0:T(8,128)(2,1)S(1)}, bf16[128,1024]{1,0:T(8,128)(2,1)S(1)}, u32[]{:S(2)}, u32[]{:S(2)}) collective-permute-start(bf16[128,1024]{1,0:T(8,128)(2,1)S(1)} %copy-done.3), channel_id=1, source_target_pairs={{0,2},{2,0},{1,3},{3,1},{4,6},{6,4},{5,7},{7,5},{8,10},{10,8},{9,1... | collective-permute-start | bytes 786440 | tf_op jit(solution)/shard_map/ppermute | solution.py:22
  19.5 6.7 %collective-permute-done = bf16[128,1024]{1,0:T(8,128)(2,1)S(1)} collective-permute-done((bf16[128,1024]{1,0:T(8,128)(2,1)S(1)}, bf16[128,1024]{1,0:T(8,128)(2,1)S(1)}, u32[]{:S(2)}, u32[]{:S(2)}) %collective-permute-start) | collective-permute-done | bytes 262176 | tf_op jit(solution)/shard_map/ppermute | solution.py:22
  26.2 16.8 %all-to-all-done = bf16[16,128,512]{2,1,0:T(8,128)(2,1)S(1)} async-done(((bf16[16,128,512]{2,1,0:T(8,128)(2,1)}), bf16[16,128,512]{2,1,0:T(8,128)(2,1)S(1)}, u32[]{:S(2)}, u32[]{:S(2)}) %all-to-all-start) | async-done | bytes 2097184 | tf_op jit(solution)/shard_map/all_to_all | solution.py:91
  43.3 0.6 fusion.1
  43.9 1.7 collective-permute-start.1
  45.6 3.0 %collective-permute-start.2 = (f32[2,512]{1,0:T(2,128)S(1)}, f32[2,512]{1,0:T(2,128)S(1)}, u32[]{:S(2)}, u32[]{:S(2)}) collective-permute-start(f32[2,512]{1,0:T(2,128)S(1)} %pad_maximum_fusion.16), channel_id=1, source_target_pairs={{0,128},{64,192},{128,0},{192,64},{1,129},{65,193},{129,1},{193,65... | collective-permute-start | bytes 12296 | tf_op jit(solution)/shard_map/ppermute | solution.py:36
  48.6 0.7 collective-permute-start.3
  49.6 1.1 broadcast_in_dim.16
  50.7 4.3 %all-to-all-start.1 = ((bf16[16,128,256]{2,1,0:T(8,128)(2,1)}), bf16[16,128,256]{2,1,0:T(8,128)(2,1)S(1)}, u32[]{:S(2)}, u32[]{:S(2)}) async-start(bf16[16,128,256]{2,1,0:T(8,128)(2,1)} %bitcast.125), calls=%async_computation.1 | async-start | bytes 2097152 | tf_op jit(solution)/shard_map/all_to_all | solution.py:91
  55.1 5.2 %collective-permute-start.5 = (f32[2,256]{1,0:T(2,128)S(1)}, f32[2,256]{1,0:T(2,128)S(1)}, u32[]{:S(2)}, u32[]{:S(2)}) collective-permute-start(f32[2,256]{1,0:T(2,128)S(1)} %pad_maximum_fusion.17), channel_id=1, source_target_pairs={{0,2},{2,0},{1,3},{3,1},{4,6},{6,4},{5,7},{7,5},{8,10},{10,8},{9,1... | collective-permute-start | bytes 6152 | tf_op jit(solution)/shard_map/ppermute | solution.py:22
  60.3 0.8 convert_reduce_fusion.2
  61.1 2.7 %collective-permute-start.6 = (f32[256]{0:T(256)S(1)}, f32[256]{0:T(256)S(1)}, u32[]{:S(2)}, u32[]{:S(2)}) collective-permute-start(f32[256]{0:T(256)S(1)} %get-tuple-element.76), channel_id=1, source_target_pairs={{0,1},{1,0},{2,3},{3,2},{4,5},{5,4},{6,7},{7,6},{8,9},{9,8},{10,11... | collective-permute-start | bytes 3080 | tf_op jit(solution)/shard_map/ppermute | solution.py:22
  63.8 1.1 fusion.133
  65.2 6.0 %collective-permute-done.7 = f32[256]{0:T(256)S(1)} collective-permute-done((f32[256]{0:T(256)S(1)}, f32[256]{0:T(256)S(1)}, u32[]{:S(2)}, u32[]{:S(2)}) %collective-permute-start.7) | collective-permute-done | bytes 1056 | tf_op jit(solution)/shard_map/ppermute | solution.py:22
  71.7 2.8 %fusion.33 = bf16[512,512]{1,0:T(8,128)(2,1)S(1)} fusion(bf16[2048,256]{1,0:T(8,128)(2,1)S(1)} %fusion.6, bf16[2048,256]{1,0:T(8,128)(2,1)S(1)} %get-tuple-element.27, bf16[2048,256]{1,0:T(8,128)(2,1)} %collective-permute-done.4, bf16[2048,256]{1,0:T(8,128)(2,1)} %get-tuple-element.26), kind=kOutput, calls=%fused_computation.55 | convolution fusion | flops 1082392576 | bytes 4718592 | tf_op jit(solution)/shard_map/dot_general | solution.py:16
  74.5 0.9 pad_maximum_fusion.14
  75.4 3.5 %all-to-all-start.2 = ((bf16[4,144,512]{2,1,0:T(8,128)(2,1)}), bf16[4,144,512]{2,1,0:T(8,128)(2,1)S(1)}, u32[]{:S(2)}, u32[]{:S(2)}) async-start(bf16[4,144,512]{2,1,0:T(8,128)(2,1)} %pad_maximum_fusion.14), calls=%async_computation.2 | async-start | bytes 1179648 | tf_op jit(solution)/shard_map/all_to_all | solution.py:125
  78.9 15.3 %all-to-all-done.2 = bf16[4,144,512]{2,1,0:T(8,128)(2,1)S(1)} async-done(((bf16[4,144,512]{2,1,0:T(8,128)(2,1)}), bf16[4,144,512]{2,1,0:T(8,128)(2,1)S(1)}, u32[]{:S(2)}, u32[]{:S(2)}) %all-to-all-start.2) | async-done | bytes 589856 | tf_op jit(solution)/shard_map/all_to_all | solution.py:125
  94.4 0.8 broadcast_in_dim.18
  95.3 3.6 %all-to-all-start.3 = ((bf16[4,128,512]{2,1,0:T(8,128)(2,1)}), bf16[4,128,512]{2,1,0:T(8,128)(2,1)S(1)}, u32[]{:S(2)}, u32[]{:S(2)}) async-start(bf16[4,128,512]{2,1,0:T(8,128)(2,1)} %broadcast_in_dim.18), calls=%async_computation.3 | async-start | bytes 1048576 | tf_op jit(solution)/shard_map/all_to_all | solution.py:27
  99.1 13.6 %all-to-all-done.3 = bf16[4,128,512]{2,1,0:T(8,128)(2,1)S(1)} async-done(((bf16[4,128,512]{2,1,0:T(8,128)(2,1)}), bf16[4,128,512]{2,1,0:T(8,128)(2,1)S(1)}, u32[]{:S(2)}, u32[]{:S(2)}) %all-to-all-start.3) | async-done | bytes 524320 | tf_op jit(solution)/shard_map/all_to_all | solution.py:27
  112.7 0.6 fusion.49
  113.4 2.8 %convolution_convert_fusion = bf16[2048,512]{1,0:T(8,128)(2,1)S(1)} fusion(bf16[512,512]{1,0:T(8,128)(2,1)S(1)} %bitcast.121, bf16[2048,256]{1,0:T(8,128)(2,1)} %collective-permute-done.4, bf16[2048,256]{1,0:T(8,128)(2,1)} %get-tuple-element.26), kind=kOutput, calls=%fused_computation.9 | convolution fusion | flops 1078984704 | bytes 4718592 | tf_op jit(solution)/shard_map/dot_general | solution.py:16
  116.2 1.7 pad_maximum_fusion
  117.9 1.3 fusion.31
  119.9 1.2 copy-done.1
  121.2 1.5 collective-permute-start.8
  122.6 6.9 %all-to-all-start.4 = ((bf16[16,144,512]{2,1,0:T(8,128)(2,1)}), bf16[16,144,512]{2,1,0:T(8,128)(2,1)S(1)}, u32[]{:S(2)}, u32[]{:S(2)}) async-start(bf16[16,144,512]{2,1,0:T(8,128)(2,1)} %pad_maximum_fusion), calls=%async_computation.4 | async-start | bytes 4718592 | tf_op jit(solution)/shard_map/all_to_all | solution.py:170
  129.6 1.4 convert_element_type.354
  131.0 1.4 copy-done
  132.6 2.4 %fusion.4 = bf16[2048,256]{1,0:T(8,128)(2,1)S(1)} fusion(f32[2064,256]{1,0:T(8,128)} %copy-done, f32[2048,512]{1,0:T(8,128)} %copy-done.1), kind=kLoop, calls=%fused_computation.13 | loop fusion | flops 1048576 | bytes 5242880 | tf_op jit(solution)/shard_map/convert_element_type | solution.py:150
  135.0 1.1 pad_maximum_fusion.12
  136.1 30.4 %all-to-all-done.4 = bf16[16,144,512]{2,1,0:T(8,128)(2,1)S(1)} async-done(((bf16[16,144,512]{2,1,0:T(8,128)(2,1)}), bf16[16,144,512]{2,1,0:T(8,128)(2,1)S(1)}, u32[]{:S(2)}, u32[]{:S(2)}) %all-to-all-start.4) | async-done | bytes 2359328 | tf_op jit(solution)/shard_map/all_to_all | solution.py:170
  167.5 0.9 fusion.59
  168.4 1.2 collective-permute-start.12
  169.5 0.8 copy.59
  170.4 0.8 copy.54
  171.9 3.8 %all-to-all-start.5 = ((bf16[16,144,256]{2,1,0:T(8,128)(2,1)}), bf16[16,144,256]{2,1,0:T(8,128)(2,1)S(1)}, u32[]{:S(2)}, u32[]{:S(2)}) async-start(bf16[16,144,256]{2,1,0:T(8,128)(2,1)} %pad_maximum_fusion.12), calls=%async_computation.5 | async-start | bytes 2359296 | tf_op jit(solution)/shard_map/all_to_all | solution.py:196
  175.7 19.6 %collective-permute-done.12 = bf16[144,1024]{0,1:T(8,128)(2,1)} collective-permute-done((bf16[144,1024]{0,1:T(8,128)(2,1)}, bf16[144,1024]{0,1:T(8,128)(2,1)}, u32[]{:S(2)}, u32[]{:S(2)}) %collective-permute-start.12) | collective-permute-done | bytes 294944 | tf_op jit(solution)/shard_map/ppermute | solution.py:22
  195.3 1.1 convert_element_type.386
  196.4 0.8 fusion.63
  197.2 0.6 fusion.67
  197.8 2.4 %fusion.43 = bf16[128,1024]{1,0:T(8,128)(2,1)S(1)} fusion(bf16[128,1024]{0,1:T(8,128)(2,1)S(1)} %fusion.67, bf16[2,2,1024,1024]{3,2,1,0:T(8,128)(2,1)} %bitcast.108, s32[]{:T(128)S(6)} %select_n.34, s32[]{:T(128)S(6)} %select_n.33), kind=kOutput, calls=%fused_computation.59 | convolution fusion | flops 268566528 | bytes 2621448 | tf_op jit(solution)/shard_map/dot_general | solution.py:16
  200.3 1.2 collective-permute-start.14
  201.5 2.4 %fusion.37 = bf16[128,1024]{1,0:T(8,128)(2,1)S(1)} fusion(bf16[128,1024]{0,1:T(8,128)(2,1)S(1)} %fusion.67, bf16[2,2,1024,1024]{3,2,1,0:T(8,128)(2,1)} %bitcast.109, s32[]{:T(128)S(6)} %select_n.31, s32[]{:T(128)S(6)} %select_n.33), kind=kOutput, calls=%fused_computation.57 | convolution fusion | flops 268566528 | bytes 2621448 | tf_op jit(solution)/shard_map/dot_general | solution.py:16
  204.2 2.4 %fusion.19 = f32[128,1024]{1,0:T(8,128)S(1)} fusion(bf16[128,1024]{0,1:T(8,128)(2,1)S(1)} %fusion.67, bf16[2,2,1024,1024]{3,2,1,0:T(8,128)(2,1)} %bitcast.110, s32[]{:T(128)S(6)} %select_n.31, s32[]{:T(128)S(6)} %select_n.32), kind=kOutput, calls=%fused_computation.33 | convolution fusion | flops 268435456 | bytes 2883592 | tf_op jit(solution)/shard_map/dot_general | solution.py:16
  207.1 0.5 copy-done.6
  207.6 0.6 fusion.70
  208.2 2.4 %fusion.40 = bf16[128,1024]{1,0:T(8,128)(2,1)S(1)} fusion(bf16[128,1024]{0,1:T(8,128)(2,1)S(1)} %fusion.70, bf16[2,2,1024,1024]{3,2,1,0:T(8,128)(2,1)} %bitcast.111, s32[]{:T(128)S(6)} %select_n.34, s32[]{:T(128)S(6)} %select_n.33), kind=kOutput, calls=%fused_computation.58 | convolution fusion | flops 268566528 | bytes 2621448 | tf_op jit(solution)/shard_map/dot_general | solution.py:16
  210.6 0.6 collective-permute-start.10
  211.2 2.4 %add_convert_fusion.1 = bf16[128,1024]{1,0:T(8,128)(2,1)S(1)} fusion(bf16[128,1024]{1,0:T(8,128)(2,1)S(1)} %collective-permute-done.14, bf16[128,1024]{0,1:T(8,128)(2,1)S(1)} %fusion.67, bf16[2,2,1024,1024]{3,2,1,0:T(8,128)(2,1)} %bitcast.112, s32[]{:T(128)S(6)} %select_n.34, s32[]{:T(128)S(6)} %select_n.32), kind=kOutput, calls=%fused_computation.98 | convolution fusion | flops 268828672 | bytes 2883592 | tf_op jit(solution)/shard_map/dot_general | solution.py:16
  213.6 3.1 %collective-permute-start.15 = (bf16[128,1024]{1,0:T(8,128)(2,1)S(1)}, bf16[128,1024]{1,0:T(8,128)(2,1)S(1)}, u32[]{:S(2)}, u32[]{:S(2)}) collective-permute-start(bf16[128,1024]{1,0:T(8,128)(2,1)S(1)} %add_convert_fusion.1), channel_id=1, source_target_pairs={{0,2},{2,0},{1,3},{3,1},{4,6},{6,4},{5,7},{7,5},{8,10},{10,8},{9,1... | collective-permute-start | bytes 786440 | tf_op jit(solution)/shard_map/ppermute | solution.py:22
  216.7 2.4 %fusion.34 = bf16[128,1024]{1,0:T(8,128)(2,1)S(1)} fusion(bf16[128,1024]{0,1:T(8,128)(2,1)S(1)} %fusion.70, bf16[2,2,1024,1024]{3,2,1,0:T(8,128)(2,1)} %bitcast.113, s32[]{:T(128)S(6)} %select_n.31, s32[]{:T(128)S(6)} %select_n.33), kind=kOutput, calls=%fused_computation.56 | convolution fusion | flops 268566528 | bytes 2621448 | tf_op jit(solution)/shard_map/dot_general | solution.py:16
  219.6 2.4 %add_convert_fusion.3 = bf16[128,1024]{1,0:T(8,128)(2,1)S(1)} fusion(bf16[128,1024]{1,0:T(8,128)(2,1)S(1)} %collective-permute-done.10, bf16[128,1024]{0,1:T(8,128)(2,1)S(1)} %fusion.70, bf16[2,2,1024,1024]{3,2,1,0:T(8,128)(2,1)} %bitcast.114, s32[]{:T(128)S(6)} %select_n.34, s32[]{:T(128)S(6)} %select_n.32), kind=kOutput, calls=%fused_computation.101 | convolution fusion | flops 268828672 | bytes 2883592 | tf_op jit(solution)/shard_map/dot_general | solution.py:16
  222.0 2.5 %collective-permute-start.11 = (bf16[128,1024]{1,0:T(8,128)(2,1)S(1)}, bf16[128,1024]{1,0:T(8,128)(2,1)S(1)}, u32[]{:S(2)}, u32[]{:S(2)}) collective-permute-start(bf16[128,1024]{1,0:T(8,128)(2,1)S(1)} %add_convert_fusion.3), channel_id=1, source_target_pairs={{0,2},{2,0},{1,3},{3,1},{4,6},{6,4},{5,7},{7,5},{8,10},{10,8},{9,1... | collective-permute-start | bytes 786440 | tf_op jit(solution)/shard_map/ppermute | solution.py:22
  224.5 6.7 %collective-permute-done.15 = bf16[128,1024]{1,0:T(8,128)(2,1)S(1)} collective-permute-done((bf16[128,1024]{1,0:T(8,128)(2,1)S(1)}, bf16[128,1024]{1,0:T(8,128)(2,1)S(1)}, u32[]{:S(2)}, u32[]{:S(2)}) %collective-permute-start.15) | collective-permute-done | bytes 262176 | tf_op jit(solution)/shard_map/ppermute | solution.py:22
  231.2 0.8 add_convert_fusion
  232.0 2.4 %fusion.21 = f32[128,1024]{1,0:T(8,128)S(1)} fusion(bf16[128,1024]{0,1:T(8,128)(2,1)S(1)} %fusion.70, bf16[2,2,1024,1024]{3,2,1,0:T(8,128)(2,1)} %bitcast.115, s32[]{:T(128)S(6)} %select_n.31, s32[]{:T(128)S(6)} %select_n.32), kind=kOutput, calls=%fused_computation.35 | convolution fusion | flops 268435456 | bytes 2883592 | tf_op jit(solution)/shard_map/dot_general | solution.py:16
  234.4 2.4 %collective-permute-done.11 = bf16[128,1024]{1,0:T(8,128)(2,1)S(1)} collective-permute-done((bf16[128,1024]{1,0:T(8,128)(2,1)S(1)}, bf16[128,1024]{1,0:T(8,128)(2,1)S(1)}, u32[]{:S(2)}, u32[]{:S(2)}) %collective-permute-start.11) | collective-permute-done | bytes 262176 | tf_op jit(solution)/shard_map/ppermute | solution.py:22
  236.8 0.8 add_convert_fusion.2
  (111 shorter events, 5.6 us)
Async XLA Ops:
  4.7 7.7 %copy-start.3 = (bf16[128,1024]{1,0:T(8,128)(2,1)S(1)}, bf16[128,1024]{1,0:T(8,128)(2,1)}, u32[]{:S(2)}) copy-start(bf16[128,1024]{1,0:T(8,128)(2,1)} %param.4) | copy-start | bytes 786436
  4.7 38.2 %all-to-all-start = ((bf16[16,128,512]{2,1,0:T(8,128)(2,1)}), bf16[16,128,512]{2,1,0:T(8,128)(2,1)S(1)}, u32[]{:S(2)}, u32[]{:S(2)}) async-start(bf16[16,128,512]{2,1,0:T(8,128)(2,1)} %bitcast.119), calls=%async_computation | async-start | bytes 4194304 | tf_op jit(solution)/shard_map/all_to_all | solution.py:91
  12.5 13.7 %collective-permute-start = (bf16[128,1024]{1,0:T(8,128)(2,1)S(1)}, bf16[128,1024]{1,0:T(8,128)(2,1)S(1)}, u32[]{:S(2)}, u32[]{:S(2)}) collective-permute-start(bf16[128,1024]{1,0:T(8,128)(2,1)S(1)} %copy-done.3), channel_id=1, source_target_pairs={{0,2},{2,0},{1,3},{3,1},{4,6},{6,4},{5,7},{7,5},{8,10},{10,8},{9,1... | collective-permute-start | bytes 786440 | tf_op jit(solution)/shard_map/ppermute | solution.py:22
  43.9 11.0 %collective-permute-start.1 = (f32[2,512]{1,0:T(2,128)S(1)}, f32[2,512]{1,0:T(2,128)S(1)}, u32[]{:S(2)}, u32[]{:S(2)}) collective-permute-start(f32[2,512]{1,0:T(2,128)S(1)} %pad_maximum_fusion.16), channel_id=1, source_target_pairs={{0,64},{64,128},{128,192},{192,0},{1,65},{65,129},{129,193},{193,1... | collective-permute-start | bytes 12296 | tf_op jit(solution)/shard_map/ppermute | solution.py:36
  45.6 9.3 %collective-permute-start.2 = (f32[2,512]{1,0:T(2,128)S(1)}, f32[2,512]{1,0:T(2,128)S(1)}, u32[]{:S(2)}, u32[]{:S(2)}) collective-permute-start(f32[2,512]{1,0:T(2,128)S(1)} %pad_maximum_fusion.16), channel_id=1, source_target_pairs={{0,128},{64,192},{128,0},{192,64},{1,129},{65,193},{129,1},{193,65... | collective-permute-start | bytes 12296 | tf_op jit(solution)/shard_map/ppermute | solution.py:36
  48.6 6.4 %collective-permute-start.3 = (f32[2,512]{1,0:T(2,128)S(1)}, f32[2,512]{1,0:T(2,128)S(1)}, u32[]{:S(2)}, u32[]{:S(2)}) collective-permute-start(f32[2,512]{1,0:T(2,128)S(1)} %pad_maximum_fusion.16), channel_id=1, source_target_pairs={{0,192},{64,0},{128,64},{192,128},{1,193},{65,1},{129,65},{193,129... | collective-permute-start | bytes 12296 | tf_op jit(solution)/shard_map/ppermute | solution.py:36
  50.7 20.6 %all-to-all-start.1 = ((bf16[16,128,256]{2,1,0:T(8,128)(2,1)}), bf16[16,128,256]{2,1,0:T(8,128)(2,1)S(1)}, u32[]{:S(2)}, u32[]{:S(2)}) async-start(bf16[16,128,256]{2,1,0:T(8,128)(2,1)} %bitcast.125), calls=%async_computation.1 | async-start | bytes 2097152 | tf_op jit(solution)/shard_map/all_to_all | solution.py:91
  55.1 16.2 %collective-permute-start.5 = (f32[2,256]{1,0:T(2,128)S(1)}, f32[2,256]{1,0:T(2,128)S(1)}, u32[]{:S(2)}, u32[]{:S(2)}) collective-permute-start(f32[2,256]{1,0:T(2,128)S(1)} %pad_maximum_fusion.17), channel_id=1, source_target_pairs={{0,2},{2,0},{1,3},{3,1},{4,6},{6,4},{5,7},{7,5},{8,10},{10,8},{9,1... | collective-permute-start | bytes 6152 | tf_op jit(solution)/shard_map/ppermute | solution.py:22
  61.1 4.1 %collective-permute-start.6 = (f32[256]{0:T(256)S(1)}, f32[256]{0:T(256)S(1)}, u32[]{:S(2)}, u32[]{:S(2)}) collective-permute-start(f32[256]{0:T(256)S(1)} %get-tuple-element.76), channel_id=1, source_target_pairs={{0,1},{1,0},{2,3},{3,2},{4,5},{5,4},{6,7},{7,6},{8,9},{9,8},{10,11... | collective-permute-start | bytes 3080 | tf_op jit(solution)/shard_map/ppermute | solution.py:22
  64.9 6.7 %collective-permute-start.4 = (bf16[2048,256]{1,0:T(8,128)(2,1)}, bf16[2048,256]{1,0:T(8,128)(2,1)}, u32[]{:S(2)}, u32[]{:S(2)}) collective-permute-start(bf16[2048,256]{1,0:T(8,128)(2,1)} %get-tuple-element.26), channel_id=1, source_target_pairs={{0,1},{1,0},{2,3},{3,2},{4,5},{5,4},{6,7},{7,6},{8,9},{9,8},{10,11... | collective-permute-start | bytes 3145736 | tf_op jit(solution)/shard_map/ppermute | solution.py:22
  64.9 6.3 %collective-permute-start.7 = (f32[256]{0:T(256)S(1)}, f32[256]{0:T(256)S(1)}, u32[]{:S(2)}, u32[]{:S(2)}) collective-permute-start(f32[256]{0:T(256)S(1)} %get-tuple-element.77), channel_id=1, source_target_pairs={{0,2},{2,0},{1,3},{3,1},{4,6},{6,4},{5,7},{7,5},{8,10},{10,8},{9,1... | collective-permute-start | bytes 3080 | tf_op jit(solution)/shard_map/ppermute | solution.py:22
  75.4 18.8 %all-to-all-start.2 = ((bf16[4,144,512]{2,1,0:T(8,128)(2,1)}), bf16[4,144,512]{2,1,0:T(8,128)(2,1)S(1)}, u32[]{:S(2)}, u32[]{:S(2)}) async-start(bf16[4,144,512]{2,1,0:T(8,128)(2,1)} %pad_maximum_fusion.14), calls=%async_computation.2 | async-start | bytes 1179648 | tf_op jit(solution)/shard_map/all_to_all | solution.py:125
  95.3 17.4 %all-to-all-start.3 = ((bf16[4,128,512]{2,1,0:T(8,128)(2,1)}), bf16[4,128,512]{2,1,0:T(8,128)(2,1)S(1)}, u32[]{:S(2)}, u32[]{:S(2)}) async-start(bf16[4,128,512]{2,1,0:T(8,128)(2,1)} %broadcast_in_dim.18), calls=%async_computation.3 | async-start | bytes 1048576 | tf_op jit(solution)/shard_map/all_to_all | solution.py:27
  119.2 1.9 copy-start.1
  121.2 8.4 %collective-permute-start.8 = (bf16[2064,256]{1,0:T(8,128)(2,1)S(1)}, bf16[2064,256]{1,0:T(8,128)(2,1)}, u32[]{:S(2)}, u32[]{:S(2)}) collective-permute-start(bf16[2064,256]{1,0:T(8,128)(2,1)S(1)} %pad_maximum_fusion.13), channel_id=1, source_target_pairs={{0,1},{1,0},{2,3},{3,2},{4,5},{5,4},{6,7},{7,6},{8,9},{9,8},{10,11... | collective-permute-start | bytes 3170312 | tf_op jit(solution)/shard_map/ppermute | solution.py:22
  122.6 43.9 %all-to-all-start.4 = ((bf16[16,144,512]{2,1,0:T(8,128)(2,1)}), bf16[16,144,512]{2,1,0:T(8,128)(2,1)S(1)}, u32[]{:S(2)}, u32[]{:S(2)}) async-start(bf16[16,144,512]{2,1,0:T(8,128)(2,1)} %pad_maximum_fusion), calls=%async_computation.4 | async-start | bytes 4718592 | tf_op jit(solution)/shard_map/all_to_all | solution.py:170
  131.0 1.4 copy-start
  166.9 2.6 %copy-start.4 = (bf16[128,1024]{1,0:T(8,128)(2,1)S(1)}, bf16[128,1024]{1,0:T(8,128)(2,1)}, u32[]{:S(2)}) copy-start(bf16[128,1024]{1,0:T(8,128)(2,1)} %param.4) | copy-start | bytes 786436
  166.9 3.5 %copy-start.5 = (bf16[128,1024]{1,0:T(8,128)(2,1)S(1)}, bf16[128,1024]{1,0:T(8,128)(2,1)}, u32[]{:S(2)}) copy-start(bf16[128,1024]{1,0:T(8,128)(2,1)} %param.3) | copy-start | bytes 786436
  168.4 26.9 %collective-permute-start.12 = (bf16[144,1024]{0,1:T(8,128)(2,1)}, bf16[144,1024]{0,1:T(8,128)(2,1)}, u32[]{:S(2)}, u32[]{:S(2)}) collective-permute-start(bf16[144,1024]{0,1:T(8,128)(2,1)} %fusion.59), channel_id=1, source_target_pairs={{0,2},{2,0},{1,3},{3,1},{4,6},{6,4},{5,7},{7,5},{8,10},{10,8},{9,1... | collective-permute-start | bytes 884744 | tf_op jit(solution)/shard_map/ppermute | solution.py:22
  171.9 34.8 %all-to-all-start.5 = ((bf16[16,144,256]{2,1,0:T(8,128)(2,1)}), bf16[16,144,256]{2,1,0:T(8,128)(2,1)S(1)}, u32[]{:S(2)}, u32[]{:S(2)}) async-start(bf16[16,144,256]{2,1,0:T(8,128)(2,1)} %pad_maximum_fusion.12), calls=%async_computation.5 | async-start | bytes 2359296 | tf_op jit(solution)/shard_map/all_to_all | solution.py:196
  175.7 21.5 %copy-start.2 = (bf16[128,1024]{0,1:T(8,128)(2,1)S(1)}, bf16[128,1024]{0,1:T(8,128)(2,1)}, u32[]{:S(2)}) copy-start(bf16[128,1024]{0,1:T(8,128)(2,1)} %copy.59) | copy-start | bytes 786436
  200.3 10.9 %collective-permute-start.14 = (bf16[128,1024]{1,0:T(8,128)(2,1)S(1)}, bf16[128,1024]{1,0:T(8,128)(2,1)S(1)}, u32[]{:S(2)}, u32[]{:S(2)}) collective-permute-start(bf16[128,1024]{1,0:T(8,128)(2,1)S(1)} %fusion.43), channel_id=1, source_target_pairs={{0,1},{1,0},{2,3},{3,2},{4,5},{5,4},{6,7},{7,6},{8,9},{9,8},{10,11... | collective-permute-start | bytes 786440 | tf_op jit(solution)/shard_map/ppermute | solution.py:22
  203.9 20.6 %collective-permute-start.13 = (bf16[128,1024]{1,0:T(8,128)(2,1)S(1)}, bf16[128,1024]{1,0:T(8,128)(2,1)S(1)}, u32[]{:S(2)}, u32[]{:S(2)}) collective-permute-start(bf16[128,1024]{1,0:T(8,128)(2,1)S(1)} %fusion.37), channel_id=1, source_target_pairs={{0,1},{1,0},{2,3},{3,2},{4,5},{5,4},{6,7},{7,6},{8,9},{9,8},{10,11... | collective-permute-start | bytes 786440 | tf_op jit(solution)/shard_map/ppermute | solution.py:22
  206.6 1.0 copy-start.6
  210.6 8.9 %collective-permute-start.10 = (bf16[128,1024]{1,0:T(8,128)(2,1)S(1)}, bf16[128,1024]{1,0:T(8,128)(2,1)S(1)}, u32[]{:S(2)}, u32[]{:S(2)}) collective-permute-start(bf16[128,1024]{1,0:T(8,128)(2,1)S(1)} %fusion.40), channel_id=1, source_target_pairs={{0,1},{1,0},{2,3},{3,2},{4,5},{5,4},{6,7},{7,6},{8,9},{9,8},{10,11... | collective-permute-start | bytes 786440 | tf_op jit(solution)/shard_map/ppermute | solution.py:22
  213.6 17.5 %collective-permute-start.15 = (bf16[128,1024]{1,0:T(8,128)(2,1)S(1)}, bf16[128,1024]{1,0:T(8,128)(2,1)S(1)}, u32[]{:S(2)}, u32[]{:S(2)}) collective-permute-start(bf16[128,1024]{1,0:T(8,128)(2,1)S(1)} %add_convert_fusion.1), channel_id=1, source_target_pairs={{0,2},{2,0},{1,3},{3,1},{4,6},{6,4},{5,7},{7,5},{8,10},{10,8},{9,1... | collective-permute-start | bytes 786440 | tf_op jit(solution)/shard_map/ppermute | solution.py:22
  219.2 15.2 %collective-permute-start.9 = (bf16[128,1024]{1,0:T(8,128)(2,1)S(1)}, bf16[128,1024]{1,0:T(8,128)(2,1)S(1)}, u32[]{:S(2)}, u32[]{:S(2)}) collective-permute-start(bf16[128,1024]{1,0:T(8,128)(2,1)S(1)} %fusion.34), channel_id=1, source_target_pairs={{0,1},{1,0},{2,3},{3,2},{4,5},{5,4},{6,7},{7,6},{8,9},{9,8},{10,11... | collective-permute-start | bytes 786440 | tf_op jit(solution)/shard_map/ppermute | solution.py:22
  222.0 14.8 %collective-permute-start.11 = (bf16[128,1024]{1,0:T(8,128)(2,1)S(1)}, bf16[128,1024]{1,0:T(8,128)(2,1)S(1)}, u32[]{:S(2)}, u32[]{:S(2)}) collective-permute-start(bf16[128,1024]{1,0:T(8,128)(2,1)S(1)} %add_convert_fusion.3), channel_id=1, source_target_pairs={{0,2},{2,0},{1,3},{3,1},{4,6},{6,4},{5,7},{7,5},{8,10},{10,8},{9,1... | collective-permute-start | bytes 786440 | tf_op jit(solution)/shard_map/ppermute | solution.py:22
